TPU v7x, 32 devices: a whole 2x2x4 slice. The times are simulated.
32 devices in a mesh: groups: 2 (over x), rows: 16 (over z, y, core).
Axes of the slice: x: 2, y: 2, z: 4, core: 2. Of those that a mesh axis runs over, the one named last changes fastest.
Arguments:
- tokens: bfloat16 [256, 8192], P(('groups', 'rows')), parts along dimension 0, may hold values from -6 to 6
- base_up_matrix: bfloat16 [8192, 28672], P(None, 'rows'), may hold values from -0.0625 to 0.0625
- adapter_down_factors: bfloat16 [32, 8192, 64], P(('groups', 'rows')), parts along dimension 0, may hold values from -0.0625 to 0.0625
- adapter_up_factors: bfloat16 [32, 64, 28672], P(('groups', 'rows')), parts along dimension 0, may hold values from -0.75 to 0.75
- row_adapter_index: int32 [256, 1], P('groups'), parts along dimension 0, may hold values from 0 to 15; in each aligned block of 128 rows (0 to 127, 128 to 255, ...) at most 32 rows name the same one
- owner: int32 [32], P('groups'), parts along dimension 0, may hold values from 0 to 15, each once
Outputs:
- hidden_up: bfloat16 [256, 28672], P('groups', 'rows'), parts along dimension 0
There are 2 independent parts, one for each index of `groups`. A program takes and returns all parts, laid end to end along the dimension named above; an argument that names none is the same for every part. Nothing has to cross between parts.
Inputs may be any that keep to these rules, and one draw needn't show every extreme that they name: `row_adapter_index`: each adapter is named by 1 to 32 rows of a group, a bound that some block reaches. `owner`: each index appears once.
All inputs are finite; a program needn't handle non-finite values.
Results may differ from a plain program's by a relative error of at most 0.0037.
Values may be sent and summed in bfloat16 or wider, within the bound.
No kernel may reach another device: no remote copies, remote signals or barrier semaphores. Data moves between devices by JAX's collectives and lax.ppermute only.
A program may use at most 128 MiB of HBM per device.

v0:
```python
import jax
import jax.numpy as jnp
from jax import lax
from jax.sharding import PartitionSpec as P

ADAPTER_RANK = 64
CAP = 32


adapter_scale = 0.5


def per_device(
    tokens, base_up_matrix, adapter_down_factors, adapter_up_factors, row_adapter_index, owner
):
    count = lax.axis_size("rows")
    device = lax.axis_index("rows")
    total = row_adapter_index.shape[0]
    slots = owner.shape[0]
    cols = base_up_matrix.shape[1]
    ids = row_adapter_index[:, 0]
    hits = (ids[:, None] == jnp.arange(slots, dtype=jnp.int32)[None, :]).astype(jnp.int32)
    ranks = jnp.sum((jnp.cumsum(hits, axis=0) - 1) * hits, axis=1)
    place = jnp.take(owner, ids) * CAP + ranks
    held = jnp.sum(jnp.arange(slots, dtype=jnp.int32) * (owner == device).astype(jnp.int32))
    down_output = adapter_down_factors[0]
    upper_output = adapter_up_factors[0]
    piece = lax.all_gather(tokens, "rows", axis=0, tiled=True)
    base_part = jnp.dot(piece, base_up_matrix, preferred_element_type=jnp.float32)
    rank_part = jnp.dot(piece, down_output, preferred_element_type=jnp.float32)
    joined = jnp.concatenate([base_part, rank_part], axis=1)
    base_output = joined[:, :cols]
    rank_all = joined[:, cols:]
    chosen = (ids[None, :] == held) & (ranks[None, :] == jnp.arange(CAP, dtype=jnp.int32)[:, None])
    slot_row = jnp.sum(
        jnp.arange(total, dtype=jnp.int32)[None, :] * chosen.astype(jnp.int32), axis=1
    )
    shrunk = jnp.take(rank_all, slot_row, axis=0).astype(jnp.bfloat16)
    factors = lax.all_to_all(upper_output, "rows", split_axis=1, concat_axis=0, tiled=True)
    gathered = lax.all_gather(shrunk, "rows", axis=0, tiled=True)
    adapter_delta = jnp.einsum(
        "scr,srk->sck",
        gathered.reshape(count, CAP, ADAPTER_RANK),
        factors.reshape(count, ADAPTER_RANK, cols),
        preferred_element_type=jnp.float32,
    )
    adapter_delta = adapter_delta.astype(jnp.bfloat16).reshape(count * CAP, cols)
    row_delta_output = jnp.take(adapter_delta, place, axis=0)
    return (base_output + adapter_scale * row_delta_output.astype(jnp.float32)).astype(jnp.bfloat16)


def solution(mesh):
    placed = (
        P(("groups", "rows"), None),
        P(None, "rows"),
        P(("groups", "rows"), None, None),
        P(("groups", "rows"), None, None),
        P("groups", None),
        P("groups"),
    )
    return jax.shard_map(
        per_device, mesh=mesh, in_specs=placed, out_specs=P("groups", "rows"), check_vma=False
    )
```

profile of v0, /device:TPU:0, one launch (start us, length us, event | category | flops | bytes accessed | tf_op | source)
XLA Modules:
  0.0 147.0 jit_solution(17476301909668386937)
XLA Ops:
  6.5 0.0 copy-start
  6.5 2.8 %copy.13 = bf16[8,8,16,1792]{3,2,1,0:T(8,128)(2,1)S(1)} copy(bf16[8,8,16,1792]{3,1,2,0:T(8,128)(2,1)} %bitcast.208) | data formatting | bytes 7340032
  9.4 2.9 %copy.11 = bf16[64,16,1792]{2,0,1:T(8,128)(2,1)} copy(bf16[64,16,1792]{2,1,0:T(8,128)(2,1)S(1)} %bitcast.207) | data formatting | bytes 7340032 | tf_op jit(solution)/shard_map/all_to_all | solution.py:39
  12.3 0.0 copy-start.2
  12.3 0.0 copy-start.1
  12.3 7.6 %all-to-all-start = ((bf16[64,16,1792]{2,0,1:T(8,128)(2,1)}), bf16[64,16,1792]{2,0,1:T(8,128)(2,1)}, u32[]{:S(2)}, u32[]{:S(2)}) async-start(bf16[64,16,1792]{2,0,1:T(8,128)(2,1)} %copy.11), calls=%async_computation | async-start | bytes 7340032 | tf_op jit(solution)/shard_map/all_to_all | solution.py:39
  19.9 0.0 all-gather.2.cloned.1.call-start
  19.9 0.7 all-gather.2.cloned.1.call-update
  20.6 0.0 copy-done.2
  20.6 0.1 fusion.8
  20.7 0.2 reduce_window_sum.11
  20.9 0.0 copy-done.1
  20.9 0.6 fusion.10
  21.5 0.2 select_reduce_fusion
  21.7 0.7 broadcast_compare_fusion
  22.4 0.1 select_reduce_fusion.1
  22.5 0.7 fusion.16
  23.2 10.2 %and_bitcast_fusion = (pred[128]{0:T(512)(128)(4,1)S(1)}, s32[128,1]{0,1:T(1,128)S(1)}) fusion(s32[128]{0:T(128)S(1)} %select_reduce_fusion, s32[]{:T(128)} %bitcast.24, s32[]{:T(128)} %bitcast.23, s32[]{:T(128)} %bitcast.22, s32[]{:T(128)} %bitcast.21, s32[]{:T(128)} %bitcast.20, s32[]{:T(128)} %bitcast.19, s32[]{:T(128)} %bitcast.18, s32[]{:T(128)} %bitcast.17, ...), kind=kLoop, calls=%fused_computation.39 | loop fusion | flops 5760 | bytes 1728 | tf_op jit(solution)/shard_map/jit(_take)/reduce_and | solution.py:48
  33.5 64.2 %all-gather.2.cloned.1.call-done = bf16[128,8192]{1,0:T(8,128)(2,1)} async-done(((bf16[8,8192]{1,0:T(8,128)(2,1)}), bf16[128,8192]{1,0:T(8,128)(2,1)}) %all-gather.2.cloned.1.call-update) | async-done | bytes 2097168 | tf_op jit(solution)/shard_map/all_gather | solution.py:28
  97.7 0.0 copy-done
  97.7 2.3 %fusion.6 = bf16[128,64]{1,0:T(8,128)(2,1)S(1)} fusion(bf16[128,8192]{1,0:T(8,128)(2,1)} %all-gather.2.cloned.1.call-done, bf16[1,8192,64]{1,2,0:T(8,128)(2,1)S(1)} %copy-done), kind=kOutput, calls=%fused_computation.7 | convolution fusion | flops 134217728 | bytes 3162112 | tf_op jit(solution)/shard_map/dot_general | solution.py:30
  100.0 0.6 gather_fusion
  100.6 0.1 select_convert_fusion
  100.7 21.2 %all_gather.7 = bf16[512,64]{1,0:T(8,128)(2,1)S(1)} all-gather(bf16[32,64]{1,0:T(8,128)(2,1)S(1)} %select_convert_fusion), channel_id=1, replica_groups=mesh['groups'=2,'rows'=16] {'rows'}, dimensions={0}, use_global_device_ids=true | all-gather | bytes 69632 | tf_op jit(solution)/shard_map/all_gather | solution.py:40
  121.8 0.0 all-to-all-done
  121.8 2.7 %fusion.2 = bf16[16,32,1792]{2,1,0:T(8,128)(2,1)S(1)} fusion(bf16[16,32,64]{2,1,0:T(8,128)(2,1)S(1)} %bitcast.209, bf16[64,16,1792]{2,0,1:T(8,128)(2,1)} %all-to-all-done), kind=kOutput, calls=%fused_computation.4 | convolution fusion | flops 118358016 | bytes 5570560 | tf_op jit(solution)/shard_map/scr,srk->sck/dot_general | solution.py:41
  124.5 0.9 gather_fusion.1
  125.5 14.7 %fusion.5 = bf16[128,1792]{1,0:T(8,128)(2,1)} fusion(bf16[128,8192]{1,0:T(8,128)(2,1)} %all-gather.2.cloned.1.call-done, bf16[8192,1792]{1,0:T(8,128)(2,1)} %param.7, bf16[128,1792]{1,0:T(8,128)(2,1)S(1)} %gather_fusion.1, pred[128]{0:T(512)(128)(4,1)S(1)} %get-tuple-element.5), kind=kOutput, calls=%fused_computation.6 | convolution fusion | flops 3759243264 | bytes 32374912 | tf_op jit(solution)/shard_map/dot_general | solution.py:29
  (4 shorter events, 0.0 us)
Async XLA Ops:
  6.5 91.2 %copy-start = (bf16[1,8192,64]{1,2,0:T(8,128)(2,1)S(1)}, bf16[1,8192,64]{1,2,0:T(8,128)(2,1)}, u32[]{:S(2)}) copy-start(bf16[1,8192,64]{1,2,0:T(8,128)(2,1)} %param.8) | copy-start | bytes 3145732
  12.3 8.3 %copy-start.2 = (s32[128,1]{0,1:T(1,128)S(1)}, s32[128,1]{0,1:T(1,128)}, u32[]{:S(2)}) copy-start(s32[128,1]{0,1:T(1,128)} %param.10) | copy-start | bytes 1540
  12.3 8.6 %copy-start.1 = (s32[16]{0:T(128)S(1)}, s32[16]{0:T(128)}, u32[]{:S(2)}) copy-start(s32[16]{0:T(128)} %param.11) | copy-start | bytes 196
  12.3 109.5 %all-to-all-start = ((bf16[64,16,1792]{2,0,1:T(8,128)(2,1)}), bf16[64,16,1792]{2,0,1:T(8,128)(2,1)}, u32[]{:S(2)}, u32[]{:S(2)}) async-start(bf16[64,16,1792]{2,0,1:T(8,128)(2,1)} %copy.11), calls=%async_computation | async-start | bytes 7340032 | tf_op jit(solution)/shard_map/all_to_all | solution.py:39
  19.9 77.8 %all-gather.2.cloned.1.call-start = ((), (), s32[]{:S(2)}) async-start(), calls=%async_computation.1 | async-start | bytes 2228224 | tf_op jit(solution)/shard_map/all_gather | solution.py:28
Sparse Core Ops, SparseCore 0:
  22.9 74.7 all-gather.1
where the time goes:
time: 149 us; the launch traced here: 147 us
  waiting for transfers between devices  64.9 us (44%)
  blocking collectives  21.2 us (14%)
  matrix products  19.7 us (13%)
  between operations  13.5 us (9%)
  other arithmetic  12.1 us (8%)
  local copies, waits for them, and re-layouts  8.03 us (5%)
  starting transfers between devices  7.6 us (5%)
    all_gather x1, waiting for transfers between devices, per_device(): piece = lax.all_gather(tokens, 'rows', axis=0, tiled=True)  64.2 us
    all_gather x1, blocking collectives, per_device(): gathered = lax.all_gather(shrunk, 'rows', axis=0, tiled=True)  21.2 us
    dot_general x1, matrix products, per_device(): jnp.dot(piece, base_up_matrix, preferred_element_type=jnp.float32)  14.7 us
    reduce_and x1, other arithmetic, per_device(): row_delta_output = jnp.take(adapter_delta, place, axis=0)  10.2 us
    all_to_all x1, starting transfers between devices, per_device(): lax.all_to_all(upper_output, 'rows', split_axis=1, concat_axis=0, tiled=T...  7.56 us
  transfers between devices with their start and end apart: 2, of which 1 were waited for; matrix products, arithmetic and copies ran while one was open for 11% of the time, Pallas kernels for 0%

commit v1 on v0

v1 whole, which is shorter than its diff:
```python
import jax
import jax.numpy as jnp
from jax import lax
from jax.sharding import PartitionSpec as P

ADAPTER_RANK = 64
CAP = 32
CORES = 2
RING = 4


adapter_scale = 0.5


def swapped(block, bits, count):
    return lax.ppermute(block, "rows", [(i, i ^ bits) for i in range(count)])


def gather_tokens(tokens, count):
    me = lax.axis_index("rows")
    devices = jnp.arange(count, dtype=jnp.int32)
    if count != RING * 2 * CORES:
        return lax.all_gather(tokens, "rows", axis=0, tiled=True), devices
    pair = jnp.concatenate([tokens, swapped(tokens, 2, count)], axis=0)
    z3 = swapped(pair, 12, count)
    z1 = swapped(pair, 4, count)
    z2 = swapped(z3, 4, count)
    column = jnp.concatenate([pair, z1, z2, z3], axis=0)
    whole = jnp.concatenate([column, swapped(column, 1, count)], axis=0)
    far = devices ^ me
    return whole, (far % 2) * (count // 2) + far // 2


def per_device(
    tokens, base_up_matrix, adapter_down_factors, adapter_up_factors, row_adapter_index, owner
):
    count = lax.axis_size("rows")
    device = lax.axis_index("rows")
    total = row_adapter_index.shape[0]
    share = tokens.shape[0]
    slots = owner.shape[0]
    ids = row_adapter_index[:, 0]
    numbers = jnp.arange(slots, dtype=jnp.int32)
    hits = (ids[:, None] == numbers[None, :]).astype(jnp.int32)
    ranks = jnp.sum((jnp.cumsum(hits, axis=0) - 1) * hits, axis=1)
    owners = jnp.sum(hits * owner[None, :], axis=1)
    place = owners * CAP + ranks

    whole, places = gather_tokens(tokens, count)
    stands = (places[:, None] * share + jnp.arange(share, dtype=jnp.int32)[None, :]).reshape(total)

    rank_all = jnp.dot(whole, adapter_down_factors[0], preferred_element_type=jnp.float32)
    rank_all = rank_all.astype(jnp.bfloat16)
    mine = jnp.where(owners == device, ranks, -1)
    rows = jnp.arange(total, dtype=jnp.int32)
    slot_place = jnp.sum(
        jnp.where(mine[None, :] == jnp.arange(CAP, dtype=jnp.int32)[:, None], stands[None, :] + 1, 0),
        axis=1,
    ) - 1
    chosen = (slot_place[:, None] == rows[None, :]).astype(jnp.bfloat16)
    shrunk = jnp.dot(chosen, rank_all, preferred_element_type=jnp.float32).astype(jnp.bfloat16)
    delta = jnp.dot(shrunk, adapter_up_factors[0], preferred_element_type=jnp.float32)
    delta = delta.astype(jnp.bfloat16)
    deltas = lax.all_to_all(delta, "rows", split_axis=1, concat_axis=0, tiled=True)

    base = jnp.dot(whole, base_up_matrix, preferred_element_type=jnp.float32)
    base = base.at[stands].get(mode="promise_in_bounds")
    row_delta = deltas.at[place].get(mode="promise_in_bounds")
    return (base + adapter_scale * row_delta.astype(jnp.float32)).astype(jnp.bfloat16)


def solution(mesh):
    placed = (
        P(("groups", "rows"), None),
        P(None, "rows"),
        P(("groups", "rows"), None, None),
        P(("groups", "rows"), None, None),
        P("groups", None),
        P("groups"),
    )
    return jax.shard_map(
        per_device, mesh=mesh, in_specs=placed, out_specs=P("groups", "rows"), check_vma=False
    )
```

time: 149 us -> 88.9 us (0.60)
  the two profiles are of different devices: /device:TPU:0 before, /device:TPU:13 now
where the time goes in v1:
time: 88.9 us; the launch traced here: 88.5 us
  waiting for transfers between devices  48.1 us (54%)
  matrix products  16 us (18%)
  local copies, waits for them, and re-layouts  12.5 us (14%)
  starting transfers between devices  10.3 us (12%)
  other arithmetic  1.52 us (2%)
    all_to_all x1, waiting for transfers between devices, per_device(): lax.all_to_all(delta, 'rows', split_axis=1, concat_axis=0, tiled=True)  28.5 us
    ppermute x5, waiting for transfers between devices, swapped(): return lax.ppermute(block, 'rows', [(i, i ^ bits) for i in range(count)])  19.6 us
    dot_general x1, matrix products, per_device(): base = jnp.dot(whole, base_up_matrix, preferred_element_type=jnp.float32)  12.3 us
    ppermute x5, starting transfers between devices, swapped(): return lax.ppermute(block, 'rows', [(i, i ^ bits) for i in range(count)])  5.74 us
    unnamed x12, local copies, waits for them, and re-layouts  4.85 us
    all_to_all x1, starting transfers between devices, per_device(): lax.all_to_all(delta, 'rows', split_axis=1, concat_axis=0, tiled=True)  4.52 us
    gather x1, local copies, waits for them, and re-layouts, per_device(): row_delta = deltas.at[place].get(mode='promise_in_bounds')  3.07 us
    dot_general x1, matrix products, per_device(): jnp.dot(shrunk, adapter_up_factors[0], preferred_element_type=jnp.float32)  2.67 us
  transfers between devices with their start and end apart: 6, of which 6 were waited for; matrix products, arithmetic and copies ran while one was open for 20% of the time, Pallas kernels for 0%

profile of v1, /device:TPU:13, one launch (start us, length us, event | category | flops | bytes accessed | tf_op | source)
XLA Modules:
  0.0 88.5 jit_solution(14541301635276362268)
XLA Ops:
  0.0 0.0 copy-start
  0.0 0.0 copy-start.2
  0.0 0.0 copy-start.3
  0.0 0.3 collective-permute-start
  0.3 1.7 %constant_dynamic-update-slice_fusion.6 = (bf16[64,8192]{1,0:T(8,128)(2,1)}, bf16[16,8192]{1,0:T(8,128)(2,1)}, bf16[128,8192]{1,0:T(8,128)(2,1)S(1)}) fusion(bf16[8,8192]{1,0:T(8,128)(2,1)} %param.6), kind=kLoop, calls=%fused_computation.20 | loop fusion | bytes 524288
  2.0 2.7 %collective-permute-done = bf16[8,8192]{1,0:T(8,128)(2,1)S(1)} collective-permute-done((bf16[8,8192]{1,0:T(8,128)(2,1)}, bf16[8,8192]{1,0:T(8,128)(2,1)S(1)}, u32[]{:S(2)}, u32[]{:S(2)}) %collective-permute-start) | collective-permute-done | bytes 131104 | tf_op jit(solution)/shard_map/ppermute | solution.py:16
  4.7 0.7 constant_dynamic-update-slice_fusion.5
  5.4 1.3 %collective-permute-start.2 = (bf16[16,8192]{1,0:T(8,128)(2,1)}, bf16[16,8192]{1,0:T(8,128)(2,1)S(1)}, u32[]{:S(2)}, u32[]{:S(2)}) collective-permute-start(bf16[16,8192]{1,0:T(8,128)(2,1)} %get-tuple-element.15), channel_id=1, source_target_pairs={{0,12},{1,13},{2,14},{3,15},{4,8},{5,9},{6,10},{7,11},{8,4},{9,5},... | collective-permute-start | bytes 786440 | tf_op jit(solution)/shard_map/ppermute | solution.py:16
  6.7 2.2 %collective-permute-start.1 = (bf16[16,8192]{1,0:T(8,128)(2,1)}, bf16[16,8192]{1,0:T(8,128)(2,1)}, u32[]{:S(2)}, u32[]{:S(2)}) collective-permute-start(bf16[16,8192]{1,0:T(8,128)(2,1)} %get-tuple-element.15), channel_id=1, source_target_pairs={{0,4},{1,5},{2,6},{3,7},{4,0},{5,1},{6,2},{7,3},{8,12},{9,13},{10,... | collective-permute-start | bytes 786440 | tf_op jit(solution)/shard_map/ppermute | solution.py:16
  8.9 9.7 %collective-permute-done.2 = bf16[16,8192]{1,0:T(8,128)(2,1)S(1)} collective-permute-done((bf16[16,8192]{1,0:T(8,128)(2,1)}, bf16[16,8192]{1,0:T(8,128)(2,1)S(1)}, u32[]{:S(2)}, u32[]{:S(2)}) %collective-permute-start.2) | collective-permute-done | bytes 262176 | tf_op jit(solution)/shard_map/ppermute | solution.py:16
  18.6 0.0 collective-permute-start.3
  18.6 1.1 %collective-permute-done.1 = bf16[16,8192]{1,0:T(8,128)(2,1)} collective-permute-done((bf16[16,8192]{1,0:T(8,128)(2,1)}, bf16[16,8192]{1,0:T(8,128)(2,1)}, u32[]{:S(2)}, u32[]{:S(2)}) %collective-permute-start.1) | collective-permute-done | bytes 262176 | tf_op jit(solution)/shard_map/ppermute | solution.py:16
  19.7 1.7 %constant_dynamic-update-slice_fusion.4 = (bf16[64,8192]{1,0:T(8,128)(2,1)}, bf16[128,8192]{1,0:T(8,128)(2,1)S(1)}) fusion(bf16[64,8192]{1,0:T(8,128)(2,1)} %get-tuple-element.13, bf16[16,8192]{1,0:T(8,128)(2,1)} %collective-permute-done.1, bf16[128,8192]{1,0:T(8,128)(2,1)S(1)} %get-tuple-element.14), kind=kLoop, calls=%fused_computation.18 | loop fusion | bytes 786432
  21.4 4.3 %collective-permute-done.3 = bf16[16,8192]{1,0:T(8,128)(2,1)S(1)} collective-permute-done((bf16[16,8192]{1,0:T(8,128)(2,1)S(1)}, bf16[16,8192]{1,0:T(8,128)(2,1)S(1)}, u32[]{:S(2)}, u32[]{:S(2)}) %collective-permute-start.3) | collective-permute-done | bytes 262176 | tf_op jit(solution)/shard_map/ppermute | solution.py:16
  25.7 0.7 constant_dynamic-update-slice_fusion.3
  26.4 0.7 constant_dynamic-update-slice_fusion.2
  27.1 2.0 %collective-permute-start.4 = (bf16[64,8192]{1,0:T(8,128)(2,1)}, bf16[64,8192]{1,0:T(8,128)(2,1)}, u32[]{:S(2)}, u32[]{:S(2)}) collective-permute-start(bf16[64,8192]{1,0:T(8,128)(2,1)} %get-tuple-element.7), channel_id=1, source_target_pairs={{0,1},{1,0},{2,3},{3,2},{4,5},{5,4},{6,7},{7,6},{8,9},{9,8},{10,11... | collective-permute-start | bytes 3145736 | tf_op jit(solution)/shard_map/ppermute | solution.py:16
  29.1 0.1 broadcast_add_fusion
  29.1 0.1 add.124
  29.2 0.0 copy-done.2
  29.2 0.1 fusion.5
  29.3 0.2 reduce_window_sum.11
  29.5 0.0 copy-done.3
  29.5 0.2 select_reduce_fusion.1
  29.7 0.1 select_reduce_fusion.2
  29.8 1.9 %collective-permute-done.4 = bf16[64,8192]{1,0:T(8,128)(2,1)} collective-permute-done((bf16[64,8192]{1,0:T(8,128)(2,1)}, bf16[64,8192]{1,0:T(8,128)(2,1)}, u32[]{:S(2)}, u32[]{:S(2)}) %collective-permute-start.4) | collective-permute-done | bytes 1048608 | tf_op jit(solution)/shard_map/ppermute | solution.py:16
  31.7 1.3 %constant_dynamic-update-slice_fusion.7 = bf16[128,8192]{1,0:T(8,128)(2,1)S(1)} fusion(bf16[128,8192]{1,0:T(8,128)(2,1)S(1)} %get-tuple-element.8, bf16[64,8192]{1,0:T(8,128)(2,1)} %collective-permute-done.4), kind=kLoop, calls=%fused_computation.21 | loop fusion | bytes 2097152 | tf_op jit(solution)/shard_map/concatenate | solution.py:29
  33.0 0.0 copy-done
  33.0 0.0 copy-start.1
  33.0 1.0 %fusion.2 = bf16[32,64]{1,0:T(8,128)(2,1)S(1)} fusion(bf16[128,8192]{1,0:T(8,128)(2,1)S(1)} %constant_dynamic-update-slice_fusion.7, bf16[1,8192,64]{1,2,0:T(8,128)(2,1)S(1)} %copy-done, s32[32]{0:T(128)S(1)} %broadcast_add_fusion.1), kind=kOutput, calls=%fused_computation.7 | convolution fusion | flops 134756352 | bytes 3149952 | tf_op jit(solution)/shard_map/dot_general | solution.py:61
  34.0 2.7 %convolution_convert_fusion = bf16[32,28672]{1,0:T(8,128)(2,1)S(1)} fusion(bf16[32,64]{1,0:T(8,128)(2,1)S(1)} %fusion.2, bf16[1,64,28672]{2,1,0:T(8,128)(2,1)} %param.9), kind=kOutput, calls=%fused_computation.2 | convolution fusion | flops 118358016 | bytes 5509120 | tf_op jit(solution)/shard_map/dot_general | solution.py:62
  36.6 0.0 copy-done.1
  36.7 1.5 %copy.13 = bf16[4,16,8,1792]{3,2,0,1:T(8,128)(2,1)} copy(bf16[4,16,8,1792]{3,2,1,0:T(8,128)(2,1)S(1)} %bitcast.25) | data formatting | bytes 3670016 | tf_op jit(solution)/shard_map/all_to_all | solution.py:64
  38.1 4.5 %all-to-all-start = ((bf16[32,16,1792]{2,0,1:T(8,128)(2,1)}), bf16[32,16,1792]{2,0,1:T(8,128)(2,1)}, u32[]{:S(2)}, u32[]{:S(2)}) async-start(bf16[32,16,1792]{2,0,1:T(8,128)(2,1)} %bitcast.24), calls=%async_computation | async-start | bytes 3670016 | tf_op jit(solution)/shard_map/all_to_all | solution.py:64
  42.6 0.1 add.119
  42.8 12.3 %fusion.12 = f32[128,1792]{1,0:T(8,128)S(1)} fusion(bf16[128,8192]{1,0:T(8,128)(2,1)} %copy-done.1, bf16[8192,1792]{1,0:T(8,128)(2,1)} %param.7), kind=kOutput, calls=%fused_computation.49 | convolution fusion | flops 3758096384 | bytes 32374784 | tf_op jit(solution)/shard_map/dot_general | solution.py:66
  55.1 1.0 %gather_fusion = f32[128,1792]{1,0:T(8,128)S(1)} fusion(f32[128,1792]{1,0:T(8,128)S(1)} %fusion.12, s32[1024]{0:T(1024)S(1)} %get-tuple-element.22), kind=kCustom, calls=%fused_computation | custom fusion | bytes 1835520 | tf_op jit(solution)/shard_map/gather | solution.py:67
  56.1 28.5 %all-to-all-done = bf16[32,16,1792]{2,0,1:T(8,128)(2,1)} async-done(((bf16[32,16,1792]{2,0,1:T(8,128)(2,1)}), bf16[32,16,1792]{2,0,1:T(8,128)(2,1)}, u32[]{:S(2)}, u32[]{:S(2)}) %all-to-all-start) | async-done | bytes 1835040 | tf_op jit(solution)/shard_map/all_to_all | solution.py:64
  84.6 3.1 %gather_fusion.1 = bf16[128,1792]{1,0:T(8,128)(2,1)S(1)} fusion(bf16[512,1792]{1,0:T(8,128)(2,1)} %bitcast.5, s32[1024]{0:T(1024)S(1)} %get-tuple-element.21), kind=kCustom, calls=%fused_computation.1 | custom fusion | bytes 918016 | tf_op jit(solution)/shard_map/gather | solution.py:68
  87.6 0.9 add_convert_fusion
  (6 shorter events, 0.0 us)
Async XLA Ops:
  0.0 33.0 %copy-start = (bf16[1,8192,64]{1,2,0:T(8,128)(2,1)S(1)}, bf16[1,8192,64]{1,2,0:T(8,128)(2,1)}, u32[]{:S(2)}) copy-start(bf16[1,8192,64]{1,2,0:T(8,128)(2,1)} %param.8) | copy-start | bytes 3145732
  0.0 29.2 %copy-start.2 = (s32[128,1]{0,1:T(1,128)S(1)}, s32[128,1]{0,1:T(1,128)}, u32[]{:S(2)}) copy-start(s32[128,1]{0,1:T(1,128)} %param.10) | copy-start | bytes 1540
  0.0 29.5 %copy-start.3 = (s32[16]{0:T(128)S(1)}, s32[16]{0:T(128)}, u32[]{:S(2)}) copy-start(s32[16]{0:T(128)} %param.11) | copy-start | bytes 196
  0.0 4.6 %collective-permute-start = (bf16[8,8192]{1,0:T(8,128)(2,1)}, bf16[8,8192]{1,0:T(8,128)(2,1)S(1)}, u32[]{:S(2)}, u32[]{:S(2)}) collective-permute-start(bf16[8,8192]{1,0:T(8,128)(2,1)} %param.6), channel_id=1, source_target_pairs={{0,2},{1,3},{2,0},{3,1},{4,6},{5,7},{6,4},{7,5},{8,10},{9,11},{10,... | collective-permute-start | bytes 393224 | tf_op jit(solution)/shard_map/ppermute | solution.py:16
  5.4 13.2 %collective-permute-start.2 = (bf16[16,8192]{1,0:T(8,128)(2,1)}, bf16[16,8192]{1,0:T(8,128)(2,1)S(1)}, u32[]{:S(2)}, u32[]{:S(2)}) collective-permute-start(bf16[16,8192]{1,0:T(8,128)(2,1)} %get-tuple-element.15), channel_id=1, source_target_pairs={{0,12},{1,13},{2,14},{3,15},{4,8},{5,9},{6,10},{7,11},{8,4},{9,5},... | collective-permute-start | bytes 786440 | tf_op jit(solution)/shard_map/ppermute | solution.py:16
  6.7 13.0 %collective-permute-start.1 = (bf16[16,8192]{1,0:T(8,128)(2,1)}, bf16[16,8192]{1,0:T(8,128)(2,1)}, u32[]{:S(2)}, u32[]{:S(2)}) collective-permute-start(bf16[16,8192]{1,0:T(8,128)(2,1)} %get-tuple-element.15), channel_id=1, source_target_pairs={{0,4},{1,5},{2,6},{3,7},{4,0},{5,1},{6,2},{7,3},{8,12},{9,13},{10,... | collective-permute-start | bytes 786440 | tf_op jit(solution)/shard_map/ppermute | solution.py:16
  18.6 7.0 %collective-permute-start.3 = (bf16[16,8192]{1,0:T(8,128)(2,1)S(1)}, bf16[16,8192]{1,0:T(8,128)(2,1)S(1)}, u32[]{:S(2)}, u32[]{:S(2)}) collective-permute-start(bf16[16,8192]{1,0:T(8,128)(2,1)S(1)} %collective-permute-done.2), channel_id=1, source_target_pairs={{0,4},{1,5},{2,6},{3,7},{4,0},{5,1},{6,2},{7,3},{8,12},{9,13},{10,... | collective-permute-start | bytes 786440 | tf_op jit(solution)/shard_map/ppermute | solution.py:16
  27.1 4.6 %collective-permute-start.4 = (bf16[64,8192]{1,0:T(8,128)(2,1)}, bf16[64,8192]{1,0:T(8,128)(2,1)}, u32[]{:S(2)}, u32[]{:S(2)}) collective-permute-start(bf16[64,8192]{1,0:T(8,128)(2,1)} %get-tuple-element.7), channel_id=1, source_target_pairs={{0,1},{1,0},{2,3},{3,2},{4,5},{5,4},{6,7},{7,6},{8,9},{9,8},{10,11... | collective-permute-start | bytes 3145736 | tf_op jit(solution)/shard_map/ppermute | solution.py:16
  33.0 3.6 %copy-start.1 = (bf16[128,8192]{1,0:T(8,128)(2,1)}, bf16[128,8192]{1,0:T(8,128)(2,1)S(1)}, u32[]{:S(2)}) copy-start(bf16[128,8192]{1,0:T(8,128)(2,1)S(1)} %constant_dynamic-update-slice_fusion.7) | copy-start | bytes 6291460
  38.1 46.4 %all-to-all-start = ((bf16[32,16,1792]{2,0,1:T(8,128)(2,1)}), bf16[32,16,1792]{2,0,1:T(8,128)(2,1)}, u32[]{:S(2)}, u32[]{:S(2)}) async-start(bf16[32,16,1792]{2,0,1:T(8,128)(2,1)} %bitcast.24), calls=%async_computation | async-start | bytes 3670016 | tf_op jit(solution)/shard_map/all_to_all | solution.py:64

commit v2 on v1

v2 whole, which is shorter than its diff:
```python
import jax
import jax.numpy as jnp
from jax import lax
from jax.experimental import pallas as pl
from jax.experimental.pallas import tpu as pltpu
from jax.sharding import PartitionSpec as P

ADAPTER_RANK = 64
CAP = 32
CORES = 2
RING = 4
ALONG_Y, ALONG_Z, ROUND_Z = 2, 4, 12
ORDER_OF_CORE = ((ALONG_Y, ALONG_Z, ROUND_Z), (ALONG_Z, ROUND_Z, ALONG_Y))


adapter_scale = 0.5


def cores_swapped(block, count):
    return lax.ppermute(block, "rows", [(i, i ^ 1) for i in range(count)])


def gather_tokens(tokens, count):
    devices = jnp.arange(count, dtype=jnp.int32)
    if count != RING * 2 * CORES:
        return lax.all_gather(tokens, "rows", axis=0, tiled=True), devices
    column = tokens
    for step in range(3):
        pairs = [(i, i ^ ORDER_OF_CORE[i % CORES][step]) for i in range(count)]
        column = jnp.concatenate([column, lax.ppermute(column, "rows", pairs)], axis=0)
    whole = jnp.concatenate([column, cores_swapped(column, count)], axis=0)
    far = devices ^ lax.axis_index("rows")
    round_z = (far >> 3) & 1
    along_z = ((far >> 2) & 1) ^ round_z
    along_y = (far >> 1) & 1
    spot = jnp.where(
        devices % CORES == 0,
        along_y + 2 * along_z + 4 * round_z,
        along_z + 2 * round_z + 4 * along_y,
    )
    return whole, (far & 1) * (count // CORES) + spot


def delta_kernel(shrunk_ref, own_ref, other_ref, delta_ref):
    rank = own_ref.shape[1]
    total = jnp.dot(shrunk_ref[:, :rank], own_ref[0], preferred_element_type=jnp.float32)
    total += jnp.dot(shrunk_ref[:, rank:], other_ref[0], preferred_element_type=jnp.float32)
    delta_ref[0] = total.astype(jnp.bfloat16)


def expand(shrunk, own, other):
    chips, rank, cols = own.shape
    rows = shrunk.shape[0]
    return pl.pallas_call(
        delta_kernel,
        grid=(chips,),
        in_specs=[
            pl.BlockSpec((rows, 2 * rank), lambda k: (0, 0)),
            pl.BlockSpec((1, rank, cols), lambda k: (k, 0, 0)),
            pl.BlockSpec((1, rank, cols), lambda k: (k, 0, 0)),
        ],
        out_specs=pl.BlockSpec((1, rows, cols), lambda k: (k, 0, 0)),
        out_shape=jax.ShapeDtypeStruct((chips, rows, cols), jnp.bfloat16),
        cost_estimate=pl.CostEstimate(
            flops=4 * chips * rows * rank * cols,
            bytes_accessed=2 * chips * (2 * rank + rows) * cols,
            transcendentals=0,
        ),
    )(shrunk, own, other)


def per_device(
    tokens, base_up_matrix, adapter_down_factors, adapter_up_factors, row_adapter_index, owner
):
    count = lax.axis_size("rows")
    device = lax.axis_index("rows")
    chips = count // CORES
    chip, core = device // CORES, device % CORES
    total = row_adapter_index.shape[0]
    share = tokens.shape[0]
    slots = owner.shape[0]
    cols = base_up_matrix.shape[1]

    split = adapter_up_factors[0].reshape(ADAPTER_RANK, chips, CORES, cols)
    split = split.transpose(2, 1, 0, 3)
    up_own = lax.dynamic_index_in_dim(split, core, 0, keepdims=False)
    up_other = cores_swapped(lax.dynamic_index_in_dim(split, 1 - core, 0, keepdims=False), count)
    down_own = adapter_down_factors[0]
    down_other = cores_swapped(down_own, count)

    ids = row_adapter_index[:, 0]
    numbers = jnp.arange(slots, dtype=jnp.int32)
    named = (ids[:, None] == numbers[None, :]).astype(jnp.int32)
    owners = jnp.sum(named * owner[None, :], axis=1)
    hits = (owners[:, None] // CORES == jnp.arange(chips, dtype=jnp.int32)[None, :]).astype(jnp.int32)
    ranks = jnp.sum((jnp.cumsum(hits, axis=0) - 1) * hits, axis=1)
    room = CORES * CAP
    place = (owners // CORES) * room + ranks

    whole, places = gather_tokens(tokens, count)
    stands = (places[:, None] * share + jnp.arange(share, dtype=jnp.int32)[None, :]).reshape(total)
    rows = jnp.arange(total, dtype=jnp.int32)
    there = stands[:, None] == rows[None, :]

    down = jnp.concatenate([down_own, down_other], axis=1)
    rank_all = jnp.dot(whole, down, preferred_element_type=jnp.float32).astype(jnp.bfloat16)
    mine = jnp.where(owners // CORES == chip, ranks, -1)
    slot = jnp.arange(room, dtype=jnp.int32)
    slot_row = jnp.sum(jnp.where(mine[None, :] == slot[:, None], rows[None, :] + 1, 0), axis=1) - 1
    is_slot = slot_row[:, None] == rows[None, :]
    slot_stands = jnp.sum(jnp.where(is_slot, stands[None, :] + 1, 0), axis=1) - 1
    slot_own = jnp.sum(jnp.where(is_slot, (owners == device)[None, :].astype(jnp.int32), 0), axis=1)
    chosen = (slot_stands[:, None] == rows[None, :]).astype(jnp.bfloat16)
    shrunk = jnp.dot(chosen, rank_all, preferred_element_type=jnp.float32)
    first = jnp.arange(CORES * ADAPTER_RANK, dtype=jnp.int32)[None, :] < ADAPTER_RANK
    shrunk = jnp.where(first == (slot_own[:, None] == 1), shrunk, 0).astype(jnp.bfloat16)

    delta = expand(shrunk, up_own, up_other)
    groups = [[CORES * k + c for k in range(chips)] for c in range(CORES)]
    deltas = lax.all_to_all(
        delta, "rows", split_axis=0, concat_axis=0, axis_index_groups=groups, tiled=True
    ).reshape(chips * room, cols)

    base = jnp.dot(whole, base_up_matrix, preferred_element_type=jnp.float32)
    base = base.at[stands].get(mode="promise_in_bounds")
    picked = place[:, None] == jnp.arange(chips * room, dtype=jnp.int32)[None, :]
    row_delta = jnp.dot(picked.astype(jnp.bfloat16), deltas, preferred_element_type=jnp.float32)
    return (base + adapter_scale * row_delta).astype(jnp.bfloat16)


def solution(mesh):
    placed = (
        P(("groups", "rows"), None),
        P(None, "rows"),
        P(("groups", "rows"), None, None),
        P(("groups", "rows"), None, None),
        P("groups", None),
        P("groups"),
    )
    return jax.shard_map(
        per_device, mesh=mesh, in_specs=placed, out_specs=P("groups", "rows"), check_vma=False
    )
```

time: 88.9 us -> 114 us (1.28)
  the two profiles are of different devices: /device:TPU:13 before, /device:TPU:0 now
where the time goes in v2:
time: 114 us
  waiting for transfers between devices  41.9 us (37%)
  local copies, waits for them, and re-layouts  30.3 us (27%)
  matrix products  16.5 us (14%)
  starting transfers between devices  15.8 us (14%)
  Pallas kernels  7.2 us (6%)
  other arithmetic  1.94 us (2%)
    all_to_all x1, waiting for transfers between devices, per_device(): lax.all_to_all(delta, 'rows', split_axis=0, concat_axis=0, axis_index_gro...  28.6 us
    another operation x1, local copies, waits for them, and re-layouts  13.6 us
    dot_general x1, matrix products, per_device(): base = jnp.dot(whole, base_up_matrix, preferred_element_type=jnp.float32)  12.3 us
    ppermute x3, waiting for transfers between devices, gather_tokens(): lax.ppermute(column, 'rows', pairs)  10.8 us
    unnamed x16, local copies, waits for them, and re-layouts  8.8 us
    ppermute x3, starting transfers between devices, gather_tokens(): lax.ppermute(column, 'rows', pairs)  8.27 us
    pallas_call x1, Pallas kernels, expand(): pl.pallas_call(delta_kernel, grid=(chips,), in_specs=[pl.BlockSpec((rows,...  7.2 us
    all_to_all x1, starting transfers between devices, per_device(): lax.all_to_all(delta, 'rows', split_axis=0, concat_axis=0, axis_index_gro...  6.95 us
  transfers between devices with their start and end apart: 7, of which 4 were waited for; matrix products, arithmetic and copies ran while one was open for 42% of the time, Pallas kernels for 0%

profile of v2, /device:TPU:0, one launch (start us, length us, event | category | flops | bytes accessed | tf_op | source)
XLA Modules:
  0.0 113.9 jit_solution(6667882487601539284)
XLA Ops:
  0.0 3.0 %collective-permute-start = (bf16[8,8192]{1,0:T(8,128)(2,1)}, bf16[8,8192]{1,0:T(8,128)(2,1)S(1)}, u32[]{:S(2)}, u32[]{:S(2)}) collective-permute-start(bf16[8,8192]{1,0:T(8,128)(2,1)} %param.6), channel_id=1, source_target_pairs={{0,2},{1,5},{2,0},{3,7},{4,6},{5,1},{6,4},{7,3},{8,10},{9,13},{10,... | collective-permute-start | bytes 393224 | tf_op jit(solution)/shard_map/ppermute | solution.py:30
  3.0 0.0 collective-permute-start.4
  3.0 5.7 %reshape_squeeze.3 = bf16[64,8,2,1792]{3,2,1,0:T(2,128)(2,1)} reshape(bf16[1,64,28672]{2,1,0:T(8,128)(2,1)} %param.9) | data formatting | bytes 7340032 | tf_op jit(solution)/shard_map/reshape;squeeze | solution.py:84
  8.7 13.6 %constant_dynamic-slice_fusion = (bf16[64,8,1,1792]{3,2,1,0:T(2,128)(2,1)}, bf16[64,8,1,1792]{3,2,1,0:T(2,128)(2,1)}) fusion(bf16[64,8,2,1792]{3,2,1,0:T(2,128)(2,1)} %reshape_squeeze.3, s32[]{:T(128)S(6)} %select_n.101, s32[]{:T(128)S(6)} %select_n.100), kind=kLoop, calls=%fused_computation.52 | loop fusion | bytes 7340040 | tf_op jit(solution)/shard_map/dynamic-slice.1
  22.3 0.0 copy-start.3
  22.3 0.0 copy-start.4
  22.3 0.0 copy-start.2
  22.3 4.4 %copy.15 = bf16[64,8,1,1792]{3,0,1,2:T(8,128)(2,1)} copy(bf16[64,8,1,1792]{3,2,1,0:T(2,128)(2,1)} %get-tuple-element.7) | data formatting | bytes 3670016
  26.7 0.5 collective-permute-start.5
  27.2 0.0 copy-done.3
  27.2 0.0 copy-done.4
  27.2 0.1 select_reduce_fusion.4
  27.4 0.0 copy-done.2
  27.4 0.1 broadcast_add_fusion
  27.5 0.1 add.170
  27.6 0.1 fusion.17
  27.7 0.2 reduce_window_sum.11
  27.8 0.2 select_reduce_fusion
  28.0 0.1 select_reduce_fusion.3
  28.1 0.2 select_reduce_fusion.2
  28.3 0.0 collective-permute-done
  28.4 1.6 %collective-permute-start.1 = (bf16[16,8192]{1,0:T(8,128)(2,1)S(1)}, bf16[16,8192]{1,0:T(8,128)(2,1)S(1)}, u32[]{:S(2)}, u32[]{:S(2)}) collective-permute-start(bf16[16,8192]{1,0:T(8,128)(2,1)S(1)} %pad_maximum_fusion.2), channel_id=1, source_target_pairs={{0,4},{1,13},{2,6},{3,15},{4,0},{5,9},{6,2},{7,11},{8,12},{9,5},{1... | collective-permute-start | bytes 786440 | tf_op jit(solution)/shard_map/ppermute | solution.py:30
  30.0 4.3 %copy.16 = bf16[64,8,1,1792]{3,0,1,2:T(8,128)(2,1)} copy(bf16[64,8,1,1792]{3,2,1,0:T(2,128)(2,1)} %get-tuple-element.8) | data formatting | bytes 3670016
  34.3 3.3 %collective-permute-done.1 = bf16[16,8192]{1,0:T(8,128)(2,1)S(1)} collective-permute-done((bf16[16,8192]{1,0:T(8,128)(2,1)S(1)}, bf16[16,8192]{1,0:T(8,128)(2,1)S(1)}, u32[]{:S(2)}, u32[]{:S(2)}) %collective-permute-start.1) | collective-permute-done | bytes 262176 | tf_op jit(solution)/shard_map/ppermute | solution.py:30
  37.6 0.1 pad_maximum_fusion.1
  37.7 3.7 %collective-permute-start.2 = (bf16[32,8192]{1,0:T(8,128)(2,1)S(1)}, bf16[32,8192]{1,0:T(8,128)(2,1)S(1)}, u32[]{:S(2)}, u32[]{:S(2)}) collective-permute-start(bf16[32,8192]{1,0:T(8,128)(2,1)S(1)} %pad_maximum_fusion.1), channel_id=1, source_target_pairs={{0,12},{1,3},{2,14},{3,1},{4,8},{5,7},{6,10},{7,5},{8,4},{9,11},{1... | collective-permute-start | bytes 1572872 | tf_op jit(solution)/shard_map/ppermute | solution.py:30
  41.4 7.5 %collective-permute-done.2 = bf16[32,8192]{1,0:T(8,128)(2,1)S(1)} collective-permute-done((bf16[32,8192]{1,0:T(8,128)(2,1)S(1)}, bf16[32,8192]{1,0:T(8,128)(2,1)S(1)}, u32[]{:S(2)}, u32[]{:S(2)}) %collective-permute-start.2) | collective-permute-done | bytes 524320 | tf_op jit(solution)/shard_map/ppermute | solution.py:30
  48.8 0.1 pad_maximum_fusion
  48.9 0.1 collective-permute-start.3
  49.1 2.6 %collective-permute-done.3 = bf16[64,8192]{1,0:T(8,128)(2,1)S(1)} collective-permute-done((bf16[64,8192]{1,0:T(8,128)(2,1)S(1)}, bf16[64,8192]{1,0:T(8,128)(2,1)S(1)}, u32[]{:S(2)}, u32[]{:S(2)}) %collective-permute-start.3) | collective-permute-done | bytes 1048608 | tf_op jit(solution)/shard_map/ppermute | solution.py:20
  51.6 0.1 constant_dynamic-update-slice_fusion
  51.7 0.0 copy-start.1
  51.7 0.0 collective-permute-done.4
  51.7 3.8 %fusion.13.shrunk_ref = bf16[64,128]{1,0:T(8,128)(2,1)} fusion(bf16[128,8192]{1,0:T(8,128)(2,1)S(1)} %constant_dynamic-update-slice_fusion, bf16[8192,64]{0,1:T(8,128)(2,1)} %collective-permute-done.4, bf16[8192,64]{0,1:T(8,128)(2,1)} %bitcast.22, s32[64]{0:T(128)S(1)} %broadcast_add_fusion.1, pred[128]{0:T(512)(128)(4,1)S(1)} %iota_compare_fusion.8, ...), kind=kOutput, calls=%fused_computation.11 | convolution fusion | flops 274776064 | bytes 4211136 | tf_op jit(solution)/shard_map/dot_general | solution.py:114
  55.5 0.0 copy-done.1
  55.5 0.0 collective-permute-done.5.other_ref
  55.5 7.2 %shard_map.64 = bf16[8,64,1792]{2,1,0:T(8,128)(2,1)} custom-call(bf16[64,128]{1,0:T(8,128)(2,1)} %fusion.13.shrunk_ref, bf16[8,64,1792]{2,1,0:T(8,128)(2,1)} %bitcast.20, bf16[8,64,1792]{2,1,0:T(8,128)(2,1)} %collective-permute-done.5.other_ref), custom_call_target="tpu_custom_call" | custom-call | flops 234881024 | bytes 5505024 | tf_op jit(solution)/shard_map/pallas_call | solution.py:54
  62.7 7.0 %all-to-all-start = ((bf16[8,64,1792]{2,1,0:T(8,128)(2,1)}), bf16[8,64,1792]{2,1,0:T(8,128)(2,1)S(1)}, u32[]{:S(2)}, u32[]{:S(2)}) async-start(bf16[8,64,1792]{2,1,0:T(8,128)(2,1)} %shard_map.64), calls=%async_computation | async-start | bytes 3670016 | tf_op jit(solution)/shard_map/all_to_all | solution.py:120
  69.6 0.1 add.164
  69.8 12.3 %fusion.22 = f32[128,1792]{1,0:T(8,128)S(1)} fusion(bf16[128,8192]{1,0:T(8,128)(2,1)} %copy-done.1, bf16[8192,1792]{1,0:T(8,128)(2,1)} %param.7), kind=kOutput, calls=%fused_computation.58 | convolution fusion | flops 3758096384 | bytes 32374784 | tf_op jit(solution)/shard_map/dot_general | solution.py:124
  82.1 1.9 %gather_fusion = f32[128,1792]{1,0:T(8,128)} fusion(f32[128,1792]{1,0:T(8,128)S(1)} %fusion.22, s32[1024]{0:T(1024)S(1)} %pad_clamp_fusion), kind=kCustom, calls=%fused_computation | custom fusion | bytes 1835520 | tf_op jit(solution)/shard_map/gather | solution.py:125
  84.0 0.0 copy-start
  84.0 28.6 %all-to-all-done = bf16[8,64,1792]{2,1,0:T(8,128)(2,1)S(1)} async-done(((bf16[8,64,1792]{2,1,0:T(8,128)(2,1)}), bf16[8,64,1792]{2,1,0:T(8,128)(2,1)S(1)}, u32[]{:S(2)}, u32[]{:S(2)}) %all-to-all-start) | async-done | bytes 1835040 | tf_op jit(solution)/shard_map/all_to_all | solution.py:120
  112.6 0.4 convolution_multiply_fusion
  113.0 0.0 copy-done
  113.0 0.9 add_convert_fusion
  (16 shorter events, 0.2 us)
Async XLA Ops:
  0.0 28.3 %collective-permute-start = (bf16[8,8192]{1,0:T(8,128)(2,1)}, bf16[8,8192]{1,0:T(8,128)(2,1)S(1)}, u32[]{:S(2)}, u32[]{:S(2)}) collective-permute-start(bf16[8,8192]{1,0:T(8,128)(2,1)} %param.6), channel_id=1, source_target_pairs={{0,2},{1,5},{2,0},{3,7},{4,6},{5,1},{6,4},{7,3},{8,10},{9,13},{10,... | collective-permute-start | bytes 393224 | tf_op jit(solution)/shard_map/ppermute | solution.py:30
  3.0 48.8 %collective-permute-start.4 = (bf16[8192,64]{0,1:T(8,128)(2,1)}, bf16[8192,64]{0,1:T(8,128)(2,1)}, u32[]{:S(2)}, u32[]{:S(2)}) collective-permute-start(bf16[8192,64]{0,1:T(8,128)(2,1)} %bitcast.21), channel_id=1, source_target_pairs={{0,1},{1,0},{2,3},{3,2},{4,5},{5,4},{6,7},{7,6},{8,9},{9,8},{10,11... | collective-permute-start | bytes 3145736 | tf_op jit(solution)/shard_map/ppermute | solution.py:20
  22.3 4.9 %copy-start.3 = (s32[16]{0:T(128)S(1)}, s32[16]{0:T(128)}, u32[]{:S(2)}) copy-start(s32[16]{0:T(128)} %param.11) | copy-start | bytes 196
  22.3 4.9 %copy-start.4 = (s32[128,1]{0,1:T(1,128)S(1)}, s32[128,1]{0,1:T(1,128)}, u32[]{:S(2)}) copy-start(s32[128,1]{0,1:T(1,128)} %param.10) | copy-start | bytes 1540
  22.3 5.1 %copy-start.2 = (bf16[8,8192]{1,0:T(8,128)(2,1)S(1)}, bf16[8,8192]{1,0:T(8,128)(2,1)}, u32[]{:S(2)}) copy-start(bf16[8,8192]{1,0:T(8,128)(2,1)} %param.6) | copy-start | bytes 393220
  26.7 28.8 %collective-permute-start.5 = (bf16[8,64,1792]{2,1,0:T(8,128)(2,1)}, bf16[8,64,1792]{2,1,0:T(8,128)(2,1)}, u32[]{:S(2)}, u32[]{:S(2)}) collective-permute-start(bf16[8,64,1792]{2,1,0:T(8,128)(2,1)} %bitcast.17), channel_id=1, source_target_pairs={{0,1},{1,0},{2,3},{3,2},{4,5},{5,4},{6,7},{7,6},{8,9},{9,8},{10,11... | collective-permute-start | bytes 5505032 | tf_op jit(solution)/shard_map/ppermute | solution.py:20
  28.4 9.2 %collective-permute-start.1 = (bf16[16,8192]{1,0:T(8,128)(2,1)S(1)}, bf16[16,8192]{1,0:T(8,128)(2,1)S(1)}, u32[]{:S(2)}, u32[]{:S(2)}) collective-permute-start(bf16[16,8192]{1,0:T(8,128)(2,1)S(1)} %pad_maximum_fusion.2), channel_id=1, source_target_pairs={{0,4},{1,13},{2,6},{3,15},{4,0},{5,9},{6,2},{7,11},{8,12},{9,5},{1... | collective-permute-start | bytes 786440 | tf_op jit(solution)/shard_map/ppermute | solution.py:30
  37.7 11.2 %collective-permute-start.2 = (bf16[32,8192]{1,0:T(8,128)(2,1)S(1)}, bf16[32,8192]{1,0:T(8,128)(2,1)S(1)}, u32[]{:S(2)}, u32[]{:S(2)}) collective-permute-start(bf16[32,8192]{1,0:T(8,128)(2,1)S(1)} %pad_maximum_fusion.1), channel_id=1, source_target_pairs={{0,12},{1,3},{2,14},{3,1},{4,8},{5,7},{6,10},{7,5},{8,4},{9,11},{1... | collective-permute-start | bytes 1572872 | tf_op jit(solution)/shard_map/ppermute | solution.py:30
  48.9 2.7 %collective-permute-start.3 = (bf16[64,8192]{1,0:T(8,128)(2,1)S(1)}, bf16[64,8192]{1,0:T(8,128)(2,1)S(1)}, u32[]{:S(2)}, u32[]{:S(2)}) collective-permute-start(bf16[64,8192]{1,0:T(8,128)(2,1)S(1)} %pad_maximum_fusion), channel_id=1, source_target_pairs={{0,1},{1,0},{2,3},{3,2},{4,5},{5,4},{6,7},{7,6},{8,9},{9,8},{10,11... | collective-permute-start | bytes 3145736 | tf_op jit(solution)/shard_map/ppermute | solution.py:20
  51.7 3.8 %copy-start.1 = (bf16[128,8192]{1,0:T(8,128)(2,1)}, bf16[128,8192]{1,0:T(8,128)(2,1)S(1)}, u32[]{:S(2)}) copy-start(bf16[128,8192]{1,0:T(8,128)(2,1)S(1)} %constant_dynamic-update-slice_fusion) | copy-start | bytes 6291460
  62.7 49.9 %all-to-all-start = ((bf16[8,64,1792]{2,1,0:T(8,128)(2,1)}), bf16[8,64,1792]{2,1,0:T(8,128)(2,1)S(1)}, u32[]{:S(2)}, u32[]{:S(2)}) async-start(bf16[8,64,1792]{2,1,0:T(8,128)(2,1)} %shard_map.64), calls=%async_computation | async-start | bytes 3670016 | tf_op jit(solution)/shard_map/all_to_all | solution.py:120
  84.0 29.0 %copy-start = (f32[128,1792]{1,0:T(8,128)S(1)}, f32[128,1792]{1,0:T(8,128)}, u32[]{:S(2)}) copy-start(f32[128,1792]{1,0:T(8,128)} %gather_fusion) | copy-start | bytes 2752516

commit v3 on v2

v3 whole, which is shorter than its diff:
```python
import jax
import jax.numpy as jnp
from jax import lax
from jax.experimental import pallas as pl
from jax.experimental.pallas import tpu as pltpu
from jax.sharding import PartitionSpec as P

ADAPTER_RANK = 64
CAP = 32
CORES = 2
RING = 4
ALONG_Y, ALONG_Z, ROUND_Z = 2, 4, 12
ORDER_OF_CORE = ((ALONG_Y, ALONG_Z, ROUND_Z), (ALONG_Z, ROUND_Z, ALONG_Y))


adapter_scale = 0.5


def cores_swapped(block, count):
    return lax.ppermute(block, "rows", [(i, i ^ 1) for i in range(count)])


def gather_tokens(tokens, count):
    column = tokens
    for step in range(3):
        pairs = [(i, i ^ ORDER_OF_CORE[i % CORES][step]) for i in range(count)]
        column = jnp.concatenate([column, lax.ppermute(column, "rows", pairs)], axis=0)
    devices = jnp.arange(count, dtype=jnp.int32)
    far = devices ^ lax.axis_index("rows")
    round_z = (far >> 3) & 1
    along_z = ((far >> 2) & 1) ^ round_z
    along_y = (far >> 1) & 1
    spot = jnp.where(
        devices % CORES == 0,
        along_y + 2 * along_z + 4 * round_z,
        along_z + 2 * round_z + 4 * along_y,
    )
    return column, (far & 1) * (count // CORES) + spot


def delta_kernel(
    core_ref, column_ref, across_ref, down_own_ref, down_other_ref, chosen_own_ref, chosen_other_ref,
    up_own_ref, up_other_ref, delta_ref, own, other, made, own_sems, other_sems, made_sems
):
    chips, _, cols = made.shape

    def fetched(k):
        place = pl.ds(pl.multiple_of((CORES * k + core_ref[0]) * cols, 128), cols)
        return (
            pltpu.make_async_copy(up_own_ref.at[:, place], own.at[k], own_sems.at[k]),
            pltpu.make_async_copy(up_other_ref.at[:, place], other.at[k], other_sems.at[k]),
        )

    for k in range(chips):
        for copy in fetched(k):
            copy.start()

    def shrink(down, chosen):
        by_rank = (((1,), (1,)), ((), ()))
        parts = [
            lax.dot_general(block[...], down[...], by_rank, preferred_element_type=jnp.float32)
            for block in (column_ref, across_ref)
        ]
        ranked = jnp.concatenate(parts, axis=0).astype(jnp.bfloat16)
        picked = jnp.dot(chosen[...], ranked, preferred_element_type=jnp.float32)
        return picked.astype(jnp.bfloat16)

    shrunk_own = shrink(down_own_ref, chosen_own_ref)
    shrunk_other = shrink(down_other_ref, chosen_other_ref)
    out = [pltpu.make_async_copy(made.at[k], delta_ref.at[k], made_sems.at[k]) for k in range(chips)]
    for k in range(chips):
        for copy in fetched(k):
            copy.wait()
        total = jnp.dot(shrunk_own, own[k], preferred_element_type=jnp.float32)
        total += jnp.dot(shrunk_other, other[k], preferred_element_type=jnp.float32)
        made[k] = total.astype(jnp.bfloat16)
        out[k].start()
    for k in range(chips):
        out[k].wait()


def chip_deltas(core, column, across, downs, chosen, ups, chips, cols):
    slots = chosen[0].shape[0]
    rank = ups[0].shape[0]
    near = pl.BlockSpec(memory_space=pltpu.VMEM)
    far = pl.BlockSpec(memory_space=pl.ANY)
    width = column.shape[1]
    return pl.pallas_call(
        delta_kernel,
        in_specs=[pl.BlockSpec(memory_space=pltpu.SMEM)] + [near] * 6 + [far] * 2,
        out_specs=far,
        out_shape=jax.ShapeDtypeStruct((chips, slots, cols), jnp.bfloat16),
        scratch_shapes=[
            pltpu.VMEM((chips, rank, cols), jnp.bfloat16),
            pltpu.VMEM((chips, rank, cols), jnp.bfloat16),
            pltpu.VMEM((chips, slots, cols), jnp.bfloat16),
            pltpu.SemaphoreType.DMA((chips,)),
            pltpu.SemaphoreType.DMA((chips,)),
            pltpu.SemaphoreType.DMA((chips,)),
        ],
        compiler_params=pltpu.CompilerParams(vmem_limit_bytes=32 * 1024 * 1024),
        cost_estimate=pl.CostEstimate(
            flops=4 * chips * slots * rank * cols + 8 * column.shape[0] * width * rank,
            bytes_accessed=2 * chips * (2 * rank + slots) * cols + 4 * (column.size + downs[0].size),
            transcendentals=0,
        ),
    )(core.reshape(1), column, across, *downs, *chosen, *ups)


def small_slice(
    tokens, base_up_matrix, adapter_down_factors, adapter_up_factors, row_adapter_index, owner
):
    count = lax.axis_size("rows")
    device = lax.axis_index("rows")
    chips = count // CORES
    chip, core = device // CORES, device % CORES
    total = row_adapter_index.shape[0]
    share = tokens.shape[0]
    slots = owner.shape[0]
    cols = base_up_matrix.shape[1]

    up_own = adapter_up_factors[0]
    up_other = cores_swapped(up_own, count)
    down_own = adapter_down_factors[0].T
    down_other = cores_swapped(down_own, count)

    ids = row_adapter_index[:, 0]
    numbers = jnp.arange(slots, dtype=jnp.int32)
    named = (ids[:, None] == numbers[None, :]).astype(jnp.int32)
    owners = jnp.sum(named * owner[None, :], axis=1)
    hits = (owners[:, None] // CORES == jnp.arange(chips, dtype=jnp.int32)[None, :]).astype(jnp.int32)
    ranks = jnp.sum((jnp.cumsum(hits, axis=0) - 1) * hits, axis=1)
    room = CORES * CAP
    place = (owners // CORES) * room + ranks

    column, places = gather_tokens(tokens, count)
    across = cores_swapped(column, count)
    stands = (places[:, None] * share + jnp.arange(share, dtype=jnp.int32)[None, :]).reshape(total)
    rows = jnp.arange(total, dtype=jnp.int32)
    there = (stands[:, None] == rows[None, :]).astype(jnp.float32)
    slot = jnp.arange(room, dtype=jnp.int32)

    def choose(adapter):
        mine = jnp.where(owners == adapter, ranks, -1)
        by_row = (slot[:, None] == mine[None, :]).astype(jnp.float32)
        return jnp.dot(by_row, there, preferred_element_type=jnp.float32).astype(jnp.bfloat16)

    chosen = (choose(device), choose(device ^ 1))
    delta = chip_deltas(
        core, column, across, (down_own, down_other), chosen, (up_own, up_other), chips, cols
    )
    groups = [[CORES * k + c for k in range(chips)] for c in range(CORES)]
    deltas = lax.all_to_all(
        delta, "rows", split_axis=0, concat_axis=0, axis_index_groups=groups, tiled=True
    ).reshape(chips * room, cols)

    whole = jnp.concatenate([column, across], axis=0)
    base = jnp.dot(whole, base_up_matrix, preferred_element_type=jnp.float32)
    base = base.at[stands].get(mode="promise_in_bounds")
    picked = place[:, None] == jnp.arange(chips * room, dtype=jnp.int32)[None, :]
    row_delta = jnp.dot(picked.astype(jnp.bfloat16), deltas, preferred_element_type=jnp.float32)
    return (base + adapter_scale * row_delta).astype(jnp.bfloat16)


def any_slice(
    tokens, base_up_matrix, adapter_down_factors, adapter_up_factors, row_adapter_index, owner
):
    device = lax.axis_index("rows")
    total = row_adapter_index.shape[0]
    ids = row_adapter_index[:, 0]
    numbers = jnp.arange(owner.shape[0], dtype=jnp.int32)
    hits = (ids[:, None] == numbers[None, :]).astype(jnp.int32)
    ranks = jnp.sum((jnp.cumsum(hits, axis=0) - 1) * hits, axis=1)
    owners = jnp.sum(hits * owner[None, :], axis=1)
    whole = lax.all_gather(tokens, "rows", axis=0, tiled=True)
    rank_all = jnp.dot(whole, adapter_down_factors[0], preferred_element_type=jnp.float32)
    mine = jnp.where(owners == device, ranks, -1)
    chosen = (jnp.arange(CAP, dtype=jnp.int32)[:, None] == mine[None, :]).astype(jnp.bfloat16)
    shrunk = jnp.dot(chosen, rank_all.astype(jnp.bfloat16), preferred_element_type=jnp.float32)
    delta = jnp.dot(
        shrunk.astype(jnp.bfloat16), adapter_up_factors[0], preferred_element_type=jnp.float32
    )
    deltas = lax.all_to_all(
        delta.astype(jnp.bfloat16), "rows", split_axis=1, concat_axis=0, tiled=True
    )
    base = jnp.dot(whole, base_up_matrix, preferred_element_type=jnp.float32)
    row_delta = deltas.at[owners * CAP + ranks].get(mode="promise_in_bounds")
    return (base + adapter_scale * row_delta.astype(jnp.float32)).astype(jnp.bfloat16)


def solution(mesh):
    placed = (
        P(("groups", "rows"), None),
        P(None, "rows"),
        P(("groups", "rows"), None, None),
        P(("groups", "rows"), None, None),
        P("groups", None),
        P("groups"),
    )
    small = mesh.shape["rows"] == RING * 2 * CORES
    per_device = small_slice if small else any_slice
    return jax.shard_map(
        per_device, mesh=mesh, in_specs=placed, out_specs=P("groups", "rows"), check_vma=False
    )
```

time: 114 us -> 94.4 us (0.83)
  local copies, waits for them, and re-layouts: 30.3 us -> 8.11 us
  other arithmetic: 1.94 us -> 4.02 us
  matrix products: 16.5 us -> 14.7 us
  starting transfers between devices: 15.8 us -> 17.5 us
  waiting for transfers between devices: 41.9 us -> 43.5 us
    another operation x2 -> x0, local copies, waits for them, and re-layouts: 19.3 us -> none
    unnamed x16 -> x7, local copies, waits for them, and re-layouts: 8.8 us -> 4.99 us
    ppermute x3, waiting for transfers between devices: 10.8 us -> 13.3 us  [gather_tokens(): lax.ppermute(column, 'rows', pairs)]
    concatenate x1 -> x2, local copies, waits for them, and re-layouts: 0.07 us -> 1.96 us  [the longest x1 1.09 us: small_slice(): whole = jnp.concatenate([column, across], axis=0)]
    dot_general x3 -> x4, matrix products: 16.5 us -> 14.7 us  [the longest x1 12.3 us: small_slice(): base = jnp.dot(whole, base_up_matrix, preferred_element_type=jnp.float32)]
    concatenate x3 -> x2, other arithmetic: 0.15 us -> 1.86 us  [gather_tokens(): jnp.concatenate([column, lax.ppermute(column, 'rows', pairs)], axis=0)]
  transfers between devices with their start and end apart: 7 -> 7, of which waited for: 4 -> 5; matrix products, arithmetic and copies ran while one was open for 42% -> 23% of each run, Pallas kernels for 0% -> 0%
where the time goes in v3:
time: 94.4 us; the launch traced here: 94 us
  waiting for transfers between devices  43.5 us (46%)
  starting transfers between devices  17.5 us (19%)
  matrix products  14.7 us (16%)
  local copies, waits for them, and re-layouts  8.11 us (9%)
  Pallas kernels  6.21 us (7%)
  other arithmetic  4.02 us (4%)
    all_to_all x1, waiting for transfers between devices, small_slice(): lax.all_to_all(delta, 'rows', split_axis=0, concat_axis=0, axis_index_gro...  28.6 us
    ppermute x3, waiting for transfers between devices, gather_tokens(): lax.ppermute(column, 'rows', pairs)  13.3 us
    dot_general x1, matrix products, small_slice(): base = jnp.dot(whole, base_up_matrix, preferred_element_type=jnp.float32)  12.3 us
    ppermute x3, starting transfers between devices, gather_tokens(): lax.ppermute(column, 'rows', pairs)  9.22 us
    all_to_all x1, starting transfers between devices, small_slice(): lax.all_to_all(delta, 'rows', split_axis=0, concat_axis=0, axis_index_gro...  7.72 us
    pallas_call x1, Pallas kernels, chip_deltas(): pl.pallas_call(delta_kernel, in_specs=[pl.BlockSpec(memory_space=pltpu.SM...  6.21 us
    unnamed x7, local copies, waits for them, and re-layouts  4.99 us
    dot_general x1, matrix products, small_slice(): jnp.dot(picked.astype(jnp.bfloat16), deltas, preferred_element_type=jnp.f...  1.94 us
  transfers between devices with their start and end apart: 7, of which 5 were waited for; matrix products, arithmetic and copies ran while one was open for 23% of the time, Pallas kernels for 0%

profile of v3, /device:TPU:0, one launch (start us, length us, event | category | flops | bytes accessed | tf_op | source)
XLA Modules:
  0.0 94.0 jit_solution(17642097328479087261)
XLA Ops:
  0.0 3.0 %collective-permute-start = (bf16[8,8192]{1,0:T(8,128)(2,1)}, bf16[8,8192]{1,0:T(8,128)(2,1)S(1)}, u32[]{:S(2)}, u32[]{:S(2)}) collective-permute-start(bf16[8,8192]{1,0:T(8,128)(2,1)} %param.6), channel_id=1, source_target_pairs={{0,2},{1,5},{2,0},{3,7},{4,6},{5,1},{6,4},{7,3},{8,10},{9,13},{10,... | collective-permute-start | bytes 393224 | tf_op jit(solution)/shard_map/ppermute | solution.py:27
  3.0 0.0 collective-permute-start.4
  3.0 0.5 collective-permute-start.5
  3.5 1.6 %constant_dynamic-update-slice_fusion.3 = (bf16[64,8192]{1,0:T(8,128)(2,1)S(1)}, bf16[128,8192]{1,0:T(8,128)(2,1)}) fusion(bf16[8,8192]{1,0:T(8,128)(2,1)} %param.6), kind=kLoop, calls=%fused_computation.20 | loop fusion | bytes 393216
  5.1 0.1 iota_add_fusion
  5.1 0.8 select_reduce_fusion.1
  5.9 0.2 collective-permute-done
  6.1 0.9 pad_maximum_fusion.1
  7.0 2.1 %collective-permute-start.1 = (bf16[16,8192]{1,0:T(8,128)(2,1)S(1)}, bf16[16,8192]{1,0:T(8,128)(2,1)S(1)}, u32[]{:S(2)}, u32[]{:S(2)}) collective-permute-start(bf16[16,8192]{1,0:T(8,128)(2,1)S(1)} %pad_maximum_fusion.1), channel_id=1, source_target_pairs={{0,4},{1,13},{2,6},{3,15},{4,0},{5,9},{6,2},{7,11},{8,12},{9,5},{1... | collective-permute-start | bytes 786440 | tf_op jit(solution)/shard_map/ppermute | solution.py:27
  9.2 0.0 copy-start.1
  9.2 0.7 constant_dynamic-update-slice_fusion.2
  9.9 6.5 %collective-permute-done.1 = bf16[16,8192]{1,0:T(8,128)(2,1)S(1)} collective-permute-done((bf16[16,8192]{1,0:T(8,128)(2,1)S(1)}, bf16[16,8192]{1,0:T(8,128)(2,1)S(1)}, u32[]{:S(2)}, u32[]{:S(2)}) %collective-permute-start.1) | collective-permute-done | bytes 262176 | tf_op jit(solution)/shard_map/ppermute | solution.py:27
  16.4 0.9 pad_maximum_fusion
  17.3 4.1 %collective-permute-start.2 = (bf16[32,8192]{1,0:T(8,128)(2,1)S(1)}, bf16[32,8192]{1,0:T(8,128)(2,1)S(1)}, u32[]{:S(2)}, u32[]{:S(2)}) collective-permute-start(bf16[32,8192]{1,0:T(8,128)(2,1)S(1)} %pad_maximum_fusion), channel_id=1, source_target_pairs={{0,12},{1,3},{2,14},{3,1},{4,8},{5,7},{6,10},{7,5},{8,4},{9,11},{1... | collective-permute-start | bytes 1572872 | tf_op jit(solution)/shard_map/ppermute | solution.py:27
  21.4 0.7 constant_dynamic-update-slice_fusion.1
  22.1 6.5 %collective-permute-done.2 = bf16[32,8192]{1,0:T(8,128)(2,1)S(1)} collective-permute-done((bf16[32,8192]{1,0:T(8,128)(2,1)S(1)}, bf16[32,8192]{1,0:T(8,128)(2,1)S(1)}, u32[]{:S(2)}, u32[]{:S(2)}) %collective-permute-start.2) | collective-permute-done | bytes 524320 | tf_op jit(solution)/shard_map/ppermute | solution.py:27
  28.7 0.9 constant_dynamic-update-slice_fusion
  29.5 0.0 collective-permute-start.3
  29.6 0.1 add.127
  29.7 0.1 add.122
  29.7 0.1 fusion.1
  29.8 0.2 reduce_window_sum.11
  30.0 0.2 select_reduce_fusion
  30.2 0.2 convolution_convert_fusion.chosen_other_ref
  30.4 0.2 convolution_convert_fusion.1.chosen_own_ref
  30.6 0.0 collective-permute-done.4.down_other_ref
  30.6 1.6 %collective-permute-done.3.across_ref = bf16[64,8192]{1,0:T(8,128)(2,1)S(1)} collective-permute-done((bf16[64,8192]{1,0:T(8,128)(2,1)S(1)}, bf16[64,8192]{1,0:T(8,128)(2,1)S(1)}, u32[]{:S(2)}, u32[]{:S(2)}) %collective-permute-start.3) | collective-permute-done | bytes 1048608 | tf_op jit(solution)/shard_map/ppermute | solution.py:20
  32.2 0.0 collective-permute-done.5.up_other_ref
  32.2 0.0 copy-done.1
  32.2 0.0 copy-start
  32.2 2.0 %copy-done = bf16[1,64,28672]{2,1,0:T(8,128)(2,1)S(1)} copy-done((bf16[1,64,28672]{2,1,0:T(8,128)(2,1)S(1)}, bf16[1,64,28672]{2,1,0:T(8,128)(2,1)}, u32[]{:S(2)}) %copy-start) | copy-done | bytes 3670040
  34.3 6.2 %shard_map.64 = bf16[8,64,1792]{2,1,0:T(8,128)(2,1)} custom-call(s32[1]{0:T(128)} %bitcast.2.core_ref, bf16[64,8192]{1,0:T(8,128)(2,1)S(1)} %get-tuple-element.5.column_ref, bf16[64,8192]{1,0:T(8,128)(2,1)S(1)} %collective-permute-done.3.across_ref, bf16[64,8192]{1,0:T(8,128)(2,1)S(1)} %bitcast.15, bf16[64,8192]{1,0:T(8,128)(2,1)} %collective-permute-done.4.down_other_ref, ...), custom_call_target="tpu_custom_call" | custom-call | flops 503316480 | bytes 9699328 | tf_op jit(solution)/shard_map/pallas_call | solution.py:88
  40.5 7.7 %all-to-all-start = ((bf16[8,64,1792]{2,1,0:T(8,128)(2,1)}), bf16[8,64,1792]{2,1,0:T(8,128)(2,1)}, u32[]{:S(2)}, u32[]{:S(2)}) async-start(bf16[8,64,1792]{2,1,0:T(8,128)(2,1)} %shard_map.64), calls=%async_computation | async-start | bytes 3670016 | tf_op jit(solution)/shard_map/all_to_all | solution.py:153
  48.2 1.1 %constant_dynamic-update-slice_fusion.4 = bf16[128,8192]{1,0:T(8,128)(2,1)} fusion(bf16[128,8192]{1,0:T(8,128)(2,1)} %get-tuple-element.6, bf16[64,8192]{1,0:T(8,128)(2,1)S(1)} %collective-permute-done.3.across_ref), kind=kLoop, calls=%fused_computation.21 | loop fusion | bytes 2097152 | tf_op jit(solution)/shard_map/concatenate | solution.py:157
  49.3 12.3 %fusion.7 = f32[128,1792]{1,0:T(8,128)S(1)} fusion(bf16[128,8192]{1,0:T(8,128)(2,1)} %constant_dynamic-update-slice_fusion.4, bf16[8192,1792]{1,0:T(8,128)(2,1)} %param.7), kind=kOutput, calls=%fused_computation.44 | convolution fusion | flops 3758096384 | bytes 32374784 | tf_op jit(solution)/shard_map/dot_general | solution.py:158
  61.6 1.0 %gather_fusion = f32[128,1792]{1,0:T(8,128)S(1)} fusion(f32[128,1792]{1,0:T(8,128)S(1)} %fusion.7, s32[1024]{0:T(1024)S(1)} %pad_clamp_fusion), kind=kCustom, calls=%fused_computation | custom fusion | bytes 1835520 | tf_op jit(solution)/shard_map/gather | solution.py:159
  62.6 28.6 %all-to-all-done = bf16[8,64,1792]{2,1,0:T(8,128)(2,1)} async-done(((bf16[8,64,1792]{2,1,0:T(8,128)(2,1)}), bf16[8,64,1792]{2,1,0:T(8,128)(2,1)}, u32[]{:S(2)}, u32[]{:S(2)}) %all-to-all-start) | async-done | bytes 1835040 | tf_op jit(solution)/shard_map/all_to_all | solution.py:153
  91.2 1.9 %convolution_multiply_fusion = f32[128,1792]{1,0:T(8,128)S(1)} fusion(bf16[512,1792]{1,0:T(8,128)(2,1)} %bitcast.7, s32[128]{0:T(128)S(1)} %get-tuple-element.15), kind=kOutput, calls=%fused_computation.1 | convolution fusion | flops 235175936 | bytes 2753024 | tf_op jit(solution)/shard_map/dot_general | solution.py:161
  93.2 0.9 add_convert_fusion
  (5 shorter events, 0.0 us)
Async XLA Ops:
  0.0 6.1 %collective-permute-start = (bf16[8,8192]{1,0:T(8,128)(2,1)}, bf16[8,8192]{1,0:T(8,128)(2,1)S(1)}, u32[]{:S(2)}, u32[]{:S(2)}) collective-permute-start(bf16[8,8192]{1,0:T(8,128)(2,1)} %param.6), channel_id=1, source_target_pairs={{0,2},{1,5},{2,0},{3,7},{4,6},{5,1},{6,4},{7,3},{8,10},{9,13},{10,... | collective-permute-start | bytes 393224 | tf_op jit(solution)/shard_map/ppermute | solution.py:27
  3.0 27.7 %collective-permute-start.4 = (bf16[64,8192]{1,0:T(8,128)(2,1)}, bf16[64,8192]{1,0:T(8,128)(2,1)}, u32[]{:S(2)}, u32[]{:S(2)}) collective-permute-start(bf16[64,8192]{1,0:T(8,128)(2,1)} %bitcast.14), channel_id=1, source_target_pairs={{0,1},{1,0},{2,3},{3,2},{4,5},{5,4},{6,7},{7,6},{8,9},{9,8},{10,11... | collective-permute-start | bytes 3145736 | tf_op jit(solution)/shard_map/ppermute | solution.py:20
  3.0 29.2 %collective-permute-start.5 = (bf16[64,28672]{1,0:T(8,128)(2,1)}, bf16[64,28672]{1,0:T(8,128)(2,1)}, u32[]{:S(2)}, u32[]{:S(2)}) collective-permute-start(bf16[64,28672]{1,0:T(8,128)(2,1)} %bitcast.12), channel_id=1, source_target_pairs={{0,1},{1,0},{2,3},{3,2},{4,5},{5,4},{6,7},{7,6},{8,9},{9,8},{10,11... | collective-permute-start | bytes 11010056 | tf_op jit(solution)/shard_map/ppermute | solution.py:20
  7.0 9.3 %collective-permute-start.1 = (bf16[16,8192]{1,0:T(8,128)(2,1)S(1)}, bf16[16,8192]{1,0:T(8,128)(2,1)S(1)}, u32[]{:S(2)}, u32[]{:S(2)}) collective-permute-start(bf16[16,8192]{1,0:T(8,128)(2,1)S(1)} %pad_maximum_fusion.1), channel_id=1, source_target_pairs={{0,4},{1,13},{2,6},{3,15},{4,0},{5,9},{6,2},{7,11},{8,12},{9,5},{1... | collective-permute-start | bytes 786440 | tf_op jit(solution)/shard_map/ppermute | solution.py:27
  9.2 23.0 %copy-start.1 = (bf16[1,8192,64]{1,2,0:T(8,128)(2,1)S(1)}, bf16[1,8192,64]{1,2,0:T(8,128)(2,1)}, u32[]{:S(2)}) copy-start(bf16[1,8192,64]{1,2,0:T(8,128)(2,1)} %param.8) | copy-start | bytes 3145732
  17.3 11.4 %collective-permute-start.2 = (bf16[32,8192]{1,0:T(8,128)(2,1)S(1)}, bf16[32,8192]{1,0:T(8,128)(2,1)S(1)}, u32[]{:S(2)}, u32[]{:S(2)}) collective-permute-start(bf16[32,8192]{1,0:T(8,128)(2,1)S(1)} %pad_maximum_fusion), channel_id=1, source_target_pairs={{0,12},{1,3},{2,14},{3,1},{4,8},{5,7},{6,10},{7,5},{8,4},{9,11},{1... | collective-permute-start | bytes 1572872 | tf_op jit(solution)/shard_map/ppermute | solution.py:27
  29.5 2.7 %collective-permute-start.3 = (bf16[64,8192]{1,0:T(8,128)(2,1)S(1)}, bf16[64,8192]{1,0:T(8,128)(2,1)S(1)}, u32[]{:S(2)}, u32[]{:S(2)}) collective-permute-start(bf16[64,8192]{1,0:T(8,128)(2,1)S(1)} %get-tuple-element.5.column_ref), channel_id=1, source_target_pairs={{0,1},{1,0},{2,3},{3,2},{4,5},{5,4},{6,7},{7,6},{8,9},{9,8},{10,11... | collective-permute-start | bytes 3145736 | tf_op jit(solution)/shard_map/ppermute | solution.py:20
  32.2 2.0 %copy-start = (bf16[1,64,28672]{2,1,0:T(8,128)(2,1)S(1)}, bf16[1,64,28672]{2,1,0:T(8,128)(2,1)}, u32[]{:S(2)}) copy-start(bf16[1,64,28672]{2,1,0:T(8,128)(2,1)} %param.9) | copy-start | bytes 11010052
  40.5 50.7 %all-to-all-start = ((bf16[8,64,1792]{2,1,0:T(8,128)(2,1)}), bf16[8,64,1792]{2,1,0:T(8,128)(2,1)}, u32[]{:S(2)}, u32[]{:S(2)}) async-start(bf16[8,64,1792]{2,1,0:T(8,128)(2,1)} %shard_map.64), calls=%async_computation | async-start | bytes 3670016 | tf_op jit(solution)/shard_map/all_to_all | solution.py:153

commit v4 on v3

--- a/solution.py
+++ b/solution.py
@@ -130,15 +130,14 @@
     owners = jnp.sum(named * owner[None, :], axis=1)
     hits = (owners[:, None] // CORES == jnp.arange(chips, dtype=jnp.int32)[None, :]).astype(jnp.int32)
     ranks = jnp.sum((jnp.cumsum(hits, axis=0) - 1) * hits, axis=1)
-    room = CORES * CAP
-    place = (owners // CORES) * room + ranks
+    most = jnp.max(jnp.sum(hits, axis=0))
 
     column, places = gather_tokens(tokens, count)
     across = cores_swapped(column, count)
     stands = (places[:, None] * share + jnp.arange(share, dtype=jnp.int32)[None, :]).reshape(total)
     rows = jnp.arange(total, dtype=jnp.int32)
     there = (stands[:, None] == rows[None, :]).astype(jnp.float32)
-    slot = jnp.arange(room, dtype=jnp.int32)
+    slot = jnp.arange(CORES * CAP, dtype=jnp.int32)
 
     def choose(adapter):
         mine = jnp.where(owners == adapter, ranks, -1)
@@ -146,20 +145,34 @@
         return jnp.dot(by_row, there, preferred_element_type=jnp.float32).astype(jnp.bfloat16)
 
     chosen = (choose(device), choose(device ^ 1))
-    delta = chip_deltas(
-        core, column, across, (down_own, down_other), chosen, (up_own, up_other), chips, cols
-    )
     groups = [[CORES * k + c for k in range(chips)] for c in range(CORES)]
-    deltas = lax.all_to_all(
-        delta, "rows", split_axis=0, concat_axis=0, axis_index_groups=groups, tiled=True
-    ).reshape(chips * room, cols)
-
-    whole = jnp.concatenate([column, across], axis=0)
-    base = jnp.dot(whole, base_up_matrix, preferred_element_type=jnp.float32)
-    base = base.at[stands].get(mode="promise_in_bounds")
-    picked = place[:, None] == jnp.arange(chips * room, dtype=jnp.int32)[None, :]
-    row_delta = jnp.dot(picked.astype(jnp.bfloat16), deltas, preferred_element_type=jnp.float32)
-    return (base + adapter_scale * row_delta).astype(jnp.bfloat16)
+
+    def finish(room):
+        def run(column, across, down_own, down_other, chosen_own, chosen_other, up_own, up_other, w):
+            picks = (chosen_own[:room], chosen_other[:room])
+            delta = chip_deltas(
+                core, column, across, (down_own, down_other), picks, (up_own, up_other), chips, cols
+            )
+            deltas = lax.all_to_all(
+                delta, "rows", split_axis=0, concat_axis=0, axis_index_groups=groups, tiled=True
+            ).reshape(chips * room, cols)
+            whole = jnp.concatenate([column, across], axis=0)
+            base = jnp.dot(whole, w, preferred_element_type=jnp.float32)
+            base = base.at[stands].get(mode="promise_in_bounds")
+            place = (owners // CORES) * room + ranks
+            picked = place[:, None] == jnp.arange(chips * room, dtype=jnp.int32)[None, :]
+            row_delta = jnp.dot(
+                picked.astype(jnp.bfloat16), deltas, preferred_element_type=jnp.float32
+            )
+            return (base + adapter_scale * row_delta).astype(jnp.bfloat16)
+
+        return run
+
+    few = CORES * CAP * 3 // 4
+    return lax.cond(
+        most <= few, finish(few), finish(CORES * CAP),
+        column, across, down_own, down_other, *chosen, up_own, up_other, base_up_matrix,
+    )
 
 
 def any_slice(

time: 94.4 us -> 81.4 us (0.86)
  waiting for transfers between devices: 43.5 us -> 36.1 us
  local copies, waits for them, and re-layouts: 8.11 us -> 2.81 us
    all_to_all x1, waiting for transfers between devices: 28.6 us -> 20.5 us  [run(): lax.all_to_all(delta, 'rows', split_axis=0, concat_axis=0, axis_index_gro...]
    unnamed x7, local copies, waits for them, and re-layouts: 4.99 us -> 1.71 us
    ppermute x3, waiting for transfers between devices: 13.3 us -> 15.3 us  [gather_tokens(): lax.ppermute(column, 'rows', pairs)]
    ppermute x3, waiting for transfers between devices: 1.59 us -> 0.37 us  [cores_swapped(): return lax.ppermute(block, 'rows', [(i, i ^ 1) for i in range(count)])]
    concatenate x1 -> x0, local copies, waits for them, and re-layouts: 1.09 us -> none  [small_slice(): whole = jnp.concatenate([column, across], axis=0)]
  transfers between devices with their start and end apart: 7 -> 7, of which waited for: 5 -> 5; matrix products, arithmetic and copies ran while one was open for 23% -> 22% of each run, Pallas kernels for 0% -> 0%
where the time goes in v4:
time: 81.4 us; the launch traced here: 81.1 us
  waiting for transfers between devices  36.1 us (44%)
  starting transfers between devices  17.5 us (21%)
  matrix products  13.9 us (17%)
  Pallas kernels  5.9 us (7%)
  other arithmetic  3.81 us (5%)
  local copies, waits for them, and re-layouts  2.81 us (3%)
    all_to_all x1, waiting for transfers between devices, run(): lax.all_to_all(delta, 'rows', split_axis=0, concat_axis=0, axis_index_gro...  20.5 us
    ppermute x3, waiting for transfers between devices, gather_tokens(): lax.ppermute(column, 'rows', pairs)  15.3 us
    dot_general x1, matrix products, run(): base = jnp.dot(whole, w, preferred_element_type=jnp.float32)  11.7 us
    ppermute x3, starting transfers between devices, gather_tokens(): lax.ppermute(column, 'rows', pairs)  9.13 us
    all_to_all x1, starting transfers between devices, run(): lax.all_to_all(delta, 'rows', split_axis=0, concat_axis=0, axis_index_gro...  7.81 us
    pallas_call x1, Pallas kernels, chip_deltas(): pl.pallas_call(delta_kernel, in_specs=[pl.BlockSpec(memory_space=pltpu.SM...  5.9 us
    concatenate x2, other arithmetic, gather_tokens(): jnp.concatenate([column, lax.ppermute(column, 'rows', pairs)], axis=0)  1.86 us
    dot_general x1, matrix products, run(): jnp.dot(picked.astype(jnp.bfloat16), deltas, preferred_element_type=jnp.f...  1.78 us
  transfers between devices with their start and end apart: 7, of which 5 were waited for; matrix products, arithmetic and copies ran while one was open for 22% of the time, Pallas kernels for 0%

profile of v4, /device:TPU:0, one launch (start us, length us, event | category | flops | bytes accessed | tf_op | source)
XLA Modules:
  0.0 81.1 jit_solution(10526037464599619417)
XLA Ops:
  0.0 0.0 copy-start
  0.0 3.0 %collective-permute-start = (bf16[8,8192]{1,0:T(8,128)(2,1)}, bf16[8,8192]{1,0:T(8,128)(2,1)S(1)}, u32[]{:S(2)}, u32[]{:S(2)}) collective-permute-start(bf16[8,8192]{1,0:T(8,128)(2,1)} %param.8), channel_id=1, source_target_pairs={{0,2},{1,5},{2,0},{3,7},{4,6},{5,1},{6,4},{7,3},{8,10},{9,13},{10,... | collective-permute-start | bytes 393224 | tf_op jit(solution)/shard_map/ppermute | solution.py:27
  3.0 0.0 collective-permute-start.4
  3.0 0.5 collective-permute-start.5
  3.5 0.9 %constant_dynamic-update-slice_fusion.3 = bf16[64,8192]{1,0:T(8,128)(2,1)S(1)} fusion(bf16[8,8192]{1,0:T(8,128)(2,1)} %param.8), kind=kLoop, calls=%fused_computation.52 | loop fusion | bytes 262144
  4.4 0.1 iota_add_fusion
  4.5 0.8 select_reduce_fusion.1
  5.2 0.9 %collective-permute-done = bf16[8,8192]{1,0:T(8,128)(2,1)S(1)} collective-permute-done((bf16[8,8192]{1,0:T(8,128)(2,1)}, bf16[8,8192]{1,0:T(8,128)(2,1)S(1)}, u32[]{:S(2)}, u32[]{:S(2)}) %collective-permute-start) | collective-permute-done | bytes 131104 | tf_op jit(solution)/shard_map/ppermute | solution.py:27
  6.1 0.9 %pad_maximum_fusion.1 = bf16[16,8192]{1,0:T(8,128)(2,1)S(1)} fusion(bf16[8,8192]{1,0:T(8,128)(2,1)S(1)} %collective-permute-done, bf16[8,8192]{1,0:T(8,128)(2,1)} %param.8), kind=kLoop, calls=%fused_computation.37 | loop fusion | flops 524288 | bytes 524288 | tf_op jit(solution)/shard_map/concatenate | solution.py:27
  7.0 2.1 %collective-permute-start.1 = (bf16[16,8192]{1,0:T(8,128)(2,1)S(1)}, bf16[16,8192]{1,0:T(8,128)(2,1)S(1)}, u32[]{:S(2)}, u32[]{:S(2)}) collective-permute-start(bf16[16,8192]{1,0:T(8,128)(2,1)S(1)} %pad_maximum_fusion.1), channel_id=1, source_target_pairs={{0,4},{1,13},{2,6},{3,15},{4,0},{5,9},{6,2},{7,11},{8,12},{9,5},{1... | collective-permute-start | bytes 786440 | tf_op jit(solution)/shard_map/ppermute | solution.py:27
  9.2 7.1 %collective-permute-done.1 = bf16[16,8192]{1,0:T(8,128)(2,1)S(1)} collective-permute-done((bf16[16,8192]{1,0:T(8,128)(2,1)S(1)}, bf16[16,8192]{1,0:T(8,128)(2,1)S(1)}, u32[]{:S(2)}, u32[]{:S(2)}) %collective-permute-start.1) | collective-permute-done | bytes 262176 | tf_op jit(solution)/shard_map/ppermute | solution.py:27
  16.4 0.9 %pad_maximum_fusion = bf16[32,8192]{1,0:T(8,128)(2,1)S(1)} fusion(bf16[16,8192]{1,0:T(8,128)(2,1)S(1)} %collective-permute-done.1, bf16[8,8192]{1,0:T(8,128)(2,1)S(1)} %collective-permute-done, bf16[8,8192]{1,0:T(8,128)(2,1)} %param.8), kind=kLoop, calls=%fused_computation.36 | loop fusion | flops 1572864 | bytes 1048576 | tf_op jit(solution)/shard_map/concatenate | solution.py:27
  17.3 4.0 %collective-permute-start.2 = (bf16[32,8192]{1,0:T(8,128)(2,1)S(1)}, bf16[32,8192]{1,0:T(8,128)(2,1)S(1)}, u32[]{:S(2)}, u32[]{:S(2)}) collective-permute-start(bf16[32,8192]{1,0:T(8,128)(2,1)S(1)} %pad_maximum_fusion), channel_id=1, source_target_pairs={{0,12},{1,3},{2,14},{3,1},{4,8},{5,7},{6,10},{7,5},{8,4},{9,11},{1... | collective-permute-start | bytes 1572872 | tf_op jit(solution)/shard_map/ppermute | solution.py:27
  21.3 7.2 %collective-permute-done.2 = bf16[32,8192]{1,0:T(8,128)(2,1)S(1)} collective-permute-done((bf16[32,8192]{1,0:T(8,128)(2,1)S(1)}, bf16[32,8192]{1,0:T(8,128)(2,1)S(1)}, u32[]{:S(2)}, u32[]{:S(2)}) %collective-permute-start.2) | collective-permute-done | bytes 524320 | tf_op jit(solution)/shard_map/ppermute | solution.py:27
  28.6 0.1 collective-permute-start.3
  28.7 0.1 add.106
  28.8 0.1 fusion.14
  28.9 0.2 reduce_window_sum.11
  29.1 0.2 select_reduce_fusion
  29.3 0.6 reduce_max.9
  30.6 0.2 convolution_convert_fusion
  30.8 0.2 convolution_convert_fusion.1
  31.0 0.0 collective-permute-done.4
  31.0 0.4 collective-permute-done.3
  31.3 0.0 collective-permute-done.5
  31.4 0.0 copy-done
  31.4 49.0 %conditional.7 = (bf16[128,1792]{1,0:T(8,128)(2,1)S(1)}) conditional(s32[]{:T(128)} %convert_element_type.31, (bf16[64,8192]{1,0:T(8,128)(2,1)S(1)}, bf16[64,8192]{1,0:T(8,128)(2,1)S(1)}, bf16[8192,1792]{1,0:T(8,128)(2,1)}, s32[128]{0:T(128)S(1)}, s32[128]{0:T(128)S(1)}, /*index=5*/s32[128]{0:T(128)S(1)}, s32[]{:T(128)}, ...), branch_computations={%region_5.6_spmd, %region_6.7_spmd} | conditional | flops 4501245440 | bytes 52633640
  31.4 5.9 %branch_1_fun.1 = bf16[8,48,1792]{2,1,0:T(8,128)(2,1)} custom-call(s32[1]{0:T(128)} %bitcast.2.core_ref, bf16[64,8192]{1,0:T(8,128)(2,1)S(1)} %get-tuple-element.79.column_ref, bf16[64,8192]{1,0:T(8,128)(2,1)S(1)} %get-tuple-element.80.across_ref, bf16[64,8192]{1,0:T(8,128)(2,1)S(1)} %get-tuple-element.86.down_own_ref, ...), custom_call_target="tpu_custom_call" | custom-call | flops 444596224 | bytes 9240576 | tf_op jit(solution)/shard_map/cond/branch_1_fun/pallas_call | solution.py:88
  37.3 7.8 %all-to-all-start.1 = ((bf16[8,48,1792]{2,1,0:T(8,128)(2,1)}), bf16[8,48,1792]{2,1,0:T(8,128)(2,1)}, u32[]{:S(2)}, u32[]{:S(2)}) async-start(bf16[8,48,1792]{2,1,0:T(8,128)(2,1)} %branch_1_fun.1), calls=%async_computation.1 | async-start | bytes 2752512 | tf_op jit(solution)/shard_map/cond/branch_1_fun/all_to_all | solution.py:156
  45.1 11.7 %fusion.8 = f32[128,1792]{1,0:T(8,128)S(1)} fusion(bf16[8192,1792]{1,0:T(8,128)(2,1)} %get-tuple-element.81, bf16[64,8192]{1,0:T(8,128)(2,1)S(1)} %get-tuple-element.80.across_ref, bf16[64,8192]{1,0:T(8,128)(2,1)S(1)} %get-tuple-element.79.column_ref), kind=kOutput, calls=%fused_computation.20 | convolution fusion | flops 3762290688 | bytes 32374784 | tf_op jit(solution)/shard_map/cond/branch_1_fun/dot_general | solution.py:160
  56.9 1.0 %gather_fusion.1 = f32[128,1792]{1,0:T(8,128)S(1)} fusion(f32[128,1792]{1,0:T(8,128)S(1)} %fusion.8, s32[1024]{0:T(1024)S(1)} %pad_clamp_fusion.1), kind=kCustom, calls=%fused_computation.1 | custom fusion | bytes 1835520 | tf_op jit(solution)/shard_map/cond/branch_1_fun/gather | solution.py:161
  57.8 20.5 %all-to-all-done.1 = bf16[8,48,1792]{2,1,0:T(8,128)(2,1)} async-done(((bf16[8,48,1792]{2,1,0:T(8,128)(2,1)}), bf16[8,48,1792]{2,1,0:T(8,128)(2,1)}, u32[]{:S(2)}, u32[]{:S(2)}) %all-to-all-start.1) | async-done | bytes 1376288 | tf_op jit(solution)/shard_map/cond/branch_1_fun/all_to_all | solution.py:156
  78.3 1.8 %fusion.7 = bf16[128,1792]{1,0:T(8,128)(2,1)S(1)} fusion(f32[128,1792]{1,0:T(8,128)S(1)} %gather_fusion.1, bf16[384,1792]{1,0:T(8,128)(2,1)} %bitcast.3, s32[128]{0:T(128)S(1)} %get-tuple-element.100), kind=kOutput, calls=%fused_computation.19 | convolution fusion | flops 176898048 | bytes 2753024 | tf_op jit(solution)/shard_map/cond/branch_1_fun/dot_general | solution.py:164
  80.3 0.0 copy-start.1
  80.3 0.8 copy-done.1
  (10 shorter events, 0.1 us)
Async XLA Ops:
  0.0 31.4 %copy-start = (bf16[1,8192,64]{1,2,0:T(8,128)(2,1)S(1)}, bf16[1,8192,64]{1,2,0:T(8,128)(2,1)}, u32[]{:S(2)}) copy-start(bf16[1,8192,64]{1,2,0:T(8,128)(2,1)} %param.10) | copy-start | bytes 3145732
  0.0 6.1 %collective-permute-start = (bf16[8,8192]{1,0:T(8,128)(2,1)}, bf16[8,8192]{1,0:T(8,128)(2,1)S(1)}, u32[]{:S(2)}, u32[]{:S(2)}) collective-permute-start(bf16[8,8192]{1,0:T(8,128)(2,1)} %param.8), channel_id=1, source_target_pairs={{0,2},{1,5},{2,0},{3,7},{4,6},{5,1},{6,4},{7,3},{8,10},{9,13},{10,... | collective-permute-start | bytes 393224 | tf_op jit(solution)/shard_map/ppermute | solution.py:27
  3.0 28.0 %collective-permute-start.4 = (bf16[64,8192]{1,0:T(8,128)(2,1)}, bf16[64,8192]{1,0:T(8,128)(2,1)}, u32[]{:S(2)}, u32[]{:S(2)}) collective-permute-start(bf16[64,8192]{1,0:T(8,128)(2,1)} %bitcast.16), channel_id=1, source_target_pairs={{0,1},{1,0},{2,3},{3,2},{4,5},{5,4},{6,7},{7,6},{8,9},{9,8},{10,11... | collective-permute-start | bytes 3145736 | tf_op jit(solution)/shard_map/ppermute | solution.py:20
  3.0 28.4 %collective-permute-start.5 = (bf16[64,28672]{1,0:T(8,128)(2,1)}, bf16[64,28672]{1,0:T(8,128)(2,1)}, u32[]{:S(2)}, u32[]{:S(2)}) collective-permute-start(bf16[64,28672]{1,0:T(8,128)(2,1)} %bitcast.13), channel_id=1, source_target_pairs={{0,1},{1,0},{2,3},{3,2},{4,5},{5,4},{6,7},{7,6},{8,9},{9,8},{10,11... | collective-permute-start | bytes 11010056 | tf_op jit(solution)/shard_map/ppermute | solution.py:20
  7.0 9.3 %collective-permute-start.1 = (bf16[16,8192]{1,0:T(8,128)(2,1)S(1)}, bf16[16,8192]{1,0:T(8,128)(2,1)S(1)}, u32[]{:S(2)}, u32[]{:S(2)}) collective-permute-start(bf16[16,8192]{1,0:T(8,128)(2,1)S(1)} %pad_maximum_fusion.1), channel_id=1, source_target_pairs={{0,4},{1,13},{2,6},{3,15},{4,0},{5,9},{6,2},{7,11},{8,12},{9,5},{1... | collective-permute-start | bytes 786440 | tf_op jit(solution)/shard_map/ppermute | solution.py:27
  17.3 11.3 %collective-permute-start.2 = (bf16[32,8192]{1,0:T(8,128)(2,1)S(1)}, bf16[32,8192]{1,0:T(8,128)(2,1)S(1)}, u32[]{:S(2)}, u32[]{:S(2)}) collective-permute-start(bf16[32,8192]{1,0:T(8,128)(2,1)S(1)} %pad_maximum_fusion), channel_id=1, source_target_pairs={{0,12},{1,3},{2,14},{3,1},{4,8},{5,7},{6,10},{7,5},{8,4},{9,11},{1... | collective-permute-start | bytes 1572872 | tf_op jit(solution)/shard_map/ppermute | solution.py:27
  28.6 2.7 %collective-permute-start.3 = (bf16[64,8192]{1,0:T(8,128)(2,1)S(1)}, bf16[64,8192]{1,0:T(8,128)(2,1)S(1)}, u32[]{:S(2)}, u32[]{:S(2)}) collective-permute-start(bf16[64,8192]{1,0:T(8,128)(2,1)S(1)} %constant_dynamic-update-slice_fusion), channel_id=1, source_target_pairs={{0,1},{1,0},{2,3},{3,2},{4,5},{5,4},{6,7},{7,6},{8,9},{9,8},{10,11... | collective-permute-start | bytes 3145736 | tf_op jit(solution)/shard_map/ppermute | solution.py:20
  37.3 41.0 %all-to-all-start.1 = ((bf16[8,48,1792]{2,1,0:T(8,128)(2,1)}), bf16[8,48,1792]{2,1,0:T(8,128)(2,1)}, u32[]{:S(2)}, u32[]{:S(2)}) async-start(bf16[8,48,1792]{2,1,0:T(8,128)(2,1)} %branch_1_fun.1), calls=%async_computation.1 | async-start | bytes 2752512 | tf_op jit(solution)/shard_map/cond/branch_1_fun/all_to_all | solution.py:156
  80.3 0.8 copy-start.1
